TPU v7x, 768 devices: a whole 4x8x12 slice. The times are simulated.
768 devices in a mesh: axial: 192 (over z, y, core), azim: 4 (over x).
Axes of the slice: x: 4, y: 8, z: 12, core: 2. Of those that a mesh axis runs over, the one named last changes fastest.
Arguments:
- tet_state: bfloat16 [175, 786432], P(None, ('axial', 'azim')), may hold values from -6 to 6
- prism_state: bfloat16 [375, 786432], P(None, ('axial', 'azim')), may hold values from -6 to 6
- tet_volume: bfloat16 [175, 175], replicated, may hold values from -0.4375 to 0.4375
- prism_volume: bfloat16 [375, 375], replicated, may hold values from -0.3125 to 0.3125
- face_extrap: bfloat16 [300, 175], replicated, may hold values from -0.4375 to 0.4375
- face_lift: bfloat16 [175, 300], replicated, may hold values from -0.75 to 0.75
- wall_extrap: bfloat16 [75, 375], replicated, may hold values from -0.3125 to 0.3125
- wall_lift: bfloat16 [375, 75], replicated, may hold values from -0.75 to 0.75
- face_code: int32 [786432], P(('axial', 'azim')), may hold values from 0 to 4095, as said below
- face_count: int32 [768, 2], P(('axial', 'azim')), may hold values from 0 to 512, as said below
- face_area: float32 [786432], P(('axial', 'azim')), may hold values from 0.5 to 2
- burn_prism: int32 [393216], P(('axial', 'azim')), may hold values from 0 to 1023, as said below
- burn_owner: int32 [393216, 1], P(('axial', 'azim')), may hold values from 0 to 3; in each aligned block of 512 rows (0 to 511, 512 to 1023, ...) at most 128 rows name the same one
- burn_law: float32 [192, 4, 6], P('axial'), may hold values from 0.5 to 2
Outputs:
- tet_new: bfloat16 [175, 786432], P(None, ('axial', 'azim'))
- prism_new: bfloat16 [375, 786432], P(None, ('axial', 'azim'))
Inputs may be any that keep to these rules, and one draw needn't show every extreme that they name: `face_code`: within each partition's block of 1024 entries the codes are distinct; the first 512 are faces shared with the lower axial neighbour, the rest with the upper; upper slot s of (a, z) is the same face as lower slot s of (a+1, z). `face_count`: column 0 counts live lower slots, column 1 live upper slots; the upper count of (a, z) equals the lower count of (a+1, z); zero at the two ends of the axial range, 1 or more elsewhere; 512 is reached. `burn_prism`: distinct within each partition's block. `burn_owner`: at most 128 wall faces of one partition name one owner, and that bound is reached.
All inputs are finite; a program needn't handle non-finite values.
Results may differ from a plain program's by a relative error of at most 0.0043.
Values may be sent and summed in bfloat16 or wider, within the bound.
No kernel may reach another device: no remote copies, remote signals or barrier semaphores. Data moves between devices by JAX's collectives and lax.ppermute only.
A program may use at most 32 MiB of HBM per device.

v0:
```python
import jax
import jax.numpy as jnp
from jax import lax
from jax.sharding import PartitionSpec as P

NV = 5
TFP = 15
BW_DEV = 512
CB = 128


section_step = 0.25


def extended_2(block, sides, width):
    for axis, dim in sides:
        count = lax.axis_size(axis)
        forward = [(i, i + 1) for i in range(count - 1)]
        backward = [(target, source) for source, target in forward]
        low = lax.ppermute(
            lax.slice_in_dim(block, block.shape[dim] - width, None, axis=dim), axis, forward
        )
        high = lax.ppermute(lax.slice_in_dim(block, 0, width, axis=dim), axis, backward)
        block = jnp.concatenate([low, block, high], axis=dim)
    return block


def square_half(values):
    widened = values.astype(jnp.float32)
    return (0.5 * widened * widened).astype(jnp.bfloat16)


def on_device(
    tet_state,
    prism_state,
    tet_volume,
    prism_volume,
    face_extrap,
    face_lift,
    wall_extrap,
    wall_lift,
    face_code,
    face_count,
    face_area,
    burn_prism,
    burn_owner,
    burn_law,
):
    face_rows = wall_extrap.shape[0]
    slots = face_code.shape[0]
    capacity = slots // 2
    face_ids = jnp.arange(4, dtype=jnp.int32)
    tet_div = jnp.dot(tet_volume, square_half(tet_state), preferred_element_type=jnp.float32)
    tet_index = face_code // 4
    chosen = (face_code % 4)[None, :] == face_ids[:, None]
    columns = jnp.take(tet_state, tet_index, axis=1)
    extended = jnp.dot(face_extrap, columns, preferred_element_type=jnp.float32).reshape(
        4, face_rows, slots
    )
    left_rows = jnp.sum(
        jnp.where(chosen[:, None, :], extended, jnp.zeros_like(extended)), axis=0
    ).astype(jnp.bfloat16)
    left_grid = left_rows.reshape(face_rows, 2, capacity)
    received = extended_2(left_grid, (("axial", 1),), 1)
    right_rows = jnp.concatenate([received[:, 0:1, :], received[:, 3:4, :]], axis=1).reshape(
        face_rows, slots
    )
    normal = jnp.concatenate(
        [-jnp.ones((capacity,), jnp.float32), jnp.ones((capacity,), jnp.float32)]
    )
    slot_index = jnp.arange(capacity, dtype=jnp.int32)
    active = (slot_index[None, :] < face_count[0][:, None]).reshape(slots)
    left_wide = left_rows.astype(jnp.float32)
    right_wide = right_rows.astype(jnp.float32)
    speed = jnp.maximum(jnp.abs(left_wide), jnp.abs(right_wide))
    flux_jump = 0.25 * normal * (right_wide * right_wide - left_wide * left_wide) - 0.5 * speed * (
        right_wide - left_wide
    )
    jump_rows = (jnp.where(active, face_area, jnp.zeros_like(face_area)) * flux_jump).astype(
        jnp.bfloat16
    )
    placed = jnp.where(
        chosen[:, None, :], jump_rows[None, :, :], jnp.zeros((4, face_rows, slots), jnp.bfloat16)
    ).reshape(4 * face_rows, slots)
    tet_lift = jnp.dot(face_lift, placed, preferred_element_type=jnp.float32)
    tet_total = tet_div.at[:, tet_index].add(tet_lift)
    tet_new = (tet_state.astype(jnp.float32) - section_step * tet_total).astype(jnp.bfloat16)
    prism_div = jnp.dot(prism_volume, square_half(prism_state), preferred_element_type=jnp.float32)
    prism_columns = jnp.take(prism_state, burn_prism, axis=1)
    wall_rows = jnp.dot(wall_extrap, prism_columns, preferred_element_type=jnp.float32).astype(
        jnp.bfloat16
    )
    sectors = lax.axis_size("azim")
    owners = burn_owner[:, 0]
    owner_int = (owners[:, None] == jnp.arange(sectors, dtype=jnp.int32)[None, :]).astype(jnp.int32)
    law_table = burn_law[0]
    before = jnp.cumsum(owner_int, axis=0) - owner_int
    ranks = jnp.sum(before * owner_int, axis=1)
    position = owners * CB + ranks
    place_table = (position[:, None] == jnp.arange(sectors * CB, dtype=jnp.int32)[None, :]).astype(
        jnp.bfloat16
    )
    outgoing = jnp.dot(wall_rows, place_table, preferred_element_type=jnp.float32).astype(
        jnp.bfloat16
    )
    outgoing = outgoing.reshape(face_rows, sectors, CB)
    incoming = lax.all_to_all(outgoing, "azim", split_axis=1, concat_axis=1, tiled=True)
    sector = lax.axis_index("azim")
    own_law = lax.dynamic_index_in_dim(law_table, sector, 0, keepdims=False)
    burn_coef = own_law[0]
    inject = own_law[1:6]
    incoming_wide = incoming.reshape(NV, TFP, sectors, CB).astype(jnp.float32)
    received_squares = incoming_wide[4] * incoming_wide[4]
    patch_total = burn_coef * jnp.sum(received_squares)
    damping = 1.0 / (1.0 + patch_total / (BW_DEV * TFP))
    response = (
        inject[:, None, None, None] * (burn_coef * damping * received_squares)[None] - incoming_wide
    ).astype(jnp.bfloat16)
    returned = lax.all_to_all(
        response.reshape(face_rows, sectors, CB), "azim", split_axis=1, concat_axis=1, tiled=True
    )
    wall_jump = lax.dot_general(
        returned.reshape(face_rows, sectors * CB),
        place_table,
        (((1,), (1,)), ((), ())),
        preferred_element_type=jnp.float32,
    ).astype(jnp.bfloat16)
    prism_lift = jnp.dot(wall_lift, wall_jump, preferred_element_type=jnp.float32)
    prism_total = prism_div.at[:, burn_prism].add(prism_lift)
    prism_new = (prism_state.astype(jnp.float32) - section_step * prism_total).astype(jnp.bfloat16)
    return (tet_new, prism_new)


def solution(mesh):
    placed = (
        P(None, ("axial", "azim")),
        P(None, ("axial", "azim")),
        P(),
        P(),
        P(),
        P(),
        P(),
        P(),
        P(("axial", "azim")),
        P(("axial", "azim"), None),
        P(("axial", "azim")),
        P(("axial", "azim")),
        P(("axial", "azim"), None),
        P("axial", None, None),
    )
    return jax.shard_map(
        on_device,
        mesh=mesh,
        in_specs=placed,
        out_specs=(P(None, ("axial", "azim")), P(None, ("axial", "azim"))),
        check_vma=False,
    )
```

profile of v0, /device:TPU:1, one launch (start us, length us, event | category | flops | bytes accessed | tf_op | source)
XLA Modules:
  0.0 77.4 jit_solution(1350938624107557270)
XLA Ops:
  0.6 0.0 copy-start
  0.6 0.0 copy-start.8
  0.7 0.7 compare_select_fusion.1
  1.4 0.7 compare_and_fusion.1
  2.1 1.5 %copy.43 = bf16[375,1024]{0,1:T(8,128)(2,1)S(1)} copy(bf16[375,1024]{1,0:T(8,128)(2,1)} %param.15) | data formatting | bytes 1536000 | tf_op args[1]
  3.6 0.7 fusion.36
  4.3 1.2 %reduce-window.6 = s32[4,4,128]{2,1,0:T(4,128)S(1)} reduce-window(s32[4,4,128]{2,1,0:T(4,128)S(1)} %fusion.36, s32[]{:T(128)} %constant.57.clone.1), window={size=1x1x128 pad=0_0x0_0x127_0}, to_apply=%region_2.3 | reduce-window | flops 260096 | bytes 16388 | tf_op jit(solution)/shard_map/reduce-window
  5.5 0.2 slice_reduce_fusion
  5.7 0.2 reduce-window.9
  5.9 0.1 add_bitcast_fusion
  6.0 0.0 copy-start.13
  6.1 1.9 %gather_fusion.1 = bf16[512,375]{1,0:T(8,128)(2,1)S(1)} fusion(bf16[375,1024]{0,1:T(8,128)(2,1)S(1)} %copy.43, s32[1024]{0:T(1024)S(1)} %pad_clamp_fusion), kind=kCustom, calls=%fused_computation.1 | custom fusion | bytes 770048 | tf_op jit(solution)/shard_map/jit(_take)/gather | solution.py:89
  8.0 0.0 copy-start.9
  8.0 0.0 copy-start.5
  8.0 0.5 convolution_convert_fusion.2
  8.6 0.1 reshape.145
  8.6 0.6 copy.45
  9.3 4.8 %all-to-all-start = ((bf16[75,4,128]{2,0,1:T(8,128)(2,1)}), bf16[75,4,128]{2,0,1:T(8,128)(2,1)S(1)}, u32[]{:S(2)}, u32[]{:S(2)}) async-start(bf16[75,4,128]{2,0,1:T(8,128)(2,1)} %copy.45), calls=%async_computation | async-start | bytes 163840 | tf_op jit(solution)/shard_map/all_to_all | solution.py:107
  14.1 0.2 copy.39
  14.4 0.0 copy-start.6
  14.4 3.9 %gather_fusion = bf16[1024,175]{1,0:T(8,128)(2,1)S(1)} fusion(bf16[175,1024]{0,1:T(8,128)(2,1)S(1)} %copy.39, s32[1024]{0:T(1024)S(1)} %broadcast_clamp_fusion), kind=kCustom, calls=%fused_computation | custom fusion | bytes 720896 | tf_op jit(solution)/shard_map/jit(_take)/gather | solution.py:56
  18.3 1.5 %convolution_bitcast_fusion.1 = f32[300,1024]{1,0:T(8,128)} fusion(bf16[300,175]{0,1:T(8,128)(2,1)S(1)} %copy-done.6, bf16[1024,175]{1,0:T(8,128)(2,1)S(1)} %gather_fusion, pred[1024]{0:T(1024)(128)(4,1)S(1)} %get-tuple-element.8), kind=kOutput, calls=%fused_computation.10 | convolution fusion | flops 107699200 | bytes 1693224 | tf_op jit(solution)/shard_map/dot_general | solution.py:57
  19.9 1.4 %reshape.143 = f32[4,75,1024]{2,1,0:T(8,128)S(1)} reshape(f32[300,1024]{1,0:T(8,128)} %convolution_bitcast_fusion.1) | data formatting | bytes 2457600 | tf_op jit(solution)/shard_map/reshape | solution.py:57
  21.3 0.1 select_reduce_fusion
  21.5 0.0 copy-start.3
  21.5 0.1 convert_element_type.85
  21.6 0.0 copy-start.12
  21.6 0.0 copy-start.7
  21.6 0.9 %fusion.44 = (bf16[75,1,512]{2,1,0:T(2,128)(2,1)}, bf16[75,1,512]{2,1,0:T(2,128)(2,1)}) fusion(bf16[75,2,512]{2,1,0:T(2,128)(2,1)S(1)} %convert_element_type.85), kind=kLoop, calls=%fused_computation.83 | loop fusion | bytes 307200 | tf_op jit(solution)/shard_map/slice | solution.py:21
  22.5 4.0 %collective-permute-start = (bf16[75,1,512]{2,1,0:T(2,128)(2,1)}, bf16[75,1,512]{2,1,0:T(2,128)(2,1)}, u32[]{:S(2)}, u32[]{:S(2)}) collective-permute-start(bf16[75,1,512]{2,1,0:T(2,128)(2,1)} %get-tuple-element.10), channel_id=1, source_target_pairs={{0,4},{4,8},{8,12},{12,16},{16,20},{20,24},{24,28},{28,32},{32,36}... | collective-permute-start | bytes 230408 | tf_op jit(solution)/shard_map/ppermute | solution.py:20
  26.6 8.8 %collective-permute-start.1 = (bf16[75,1,512]{2,1,0:T(2,128)(2,1)}, bf16[75,1,512]{2,1,0:T(2,128)(2,1)}, u32[]{:S(2)}, u32[]{:S(2)}) collective-permute-start(bf16[75,1,512]{2,1,0:T(2,128)(2,1)} %get-tuple-element.11), channel_id=1, source_target_pairs={{4,0},{8,4},{12,8},{16,12},{20,16},{24,20},{28,24},{32,28},{36,32}... | collective-permute-start | bytes 230408 | tf_op jit(solution)/shard_map/ppermute | solution.py:23
  35.4 0.0 copy-start.10
  35.4 1.8 %convolution_bitcast_fusion = f32[375,1024]{1,0:T(8,128)} fusion(bf16[375,375]{1,0:T(8,128)(2,1)S(1)} %copy-done, bf16[375,1024]{0,1:T(8,128)(2,1)S(1)} %copy.43), kind=kOutput, calls=%fused_computation.9 | convolution fusion | flops 289536000 | bytes 2585250 | tf_op jit(solution)/shard_map/dot_general | solution.py:88
  37.2 0.1 iota_compare_fusion.7
  37.3 1.2 %convolution_bitcast_fusion.2 = f32[175,1024]{1,0:T(8,128)} fusion(bf16[175,175]{1,0:T(8,128)(2,1)S(1)} %copy-done.7, bf16[175,1024]{0,1:T(8,128)(2,1)S(1)} %copy.39), kind=kOutput, calls=%fused_computation.13 | convolution fusion | flops 63436800 | bytes 1136450 | tf_op jit(solution)/shard_map/dot_general | solution.py:53
  38.5 0.7 constant_dynamic-slice_fusion
  39.2 0.1 slice_bitcast_fusion
  39.2 0.1 mul.156
  39.3 0.1 mul.157
  39.4 1.9 %copy.50 = f32[375,1024]{0,1:T(8,128)S(1)} copy(f32[375,1024]{1,0:T(8,128)} %convolution_bitcast_fusion) | data formatting | bytes 3072000 | tf_op jit(solution)/shard_map/dot_general | solution.py:88
  41.3 1.4 %copy.41 = f32[175,1024]{0,1:T(8,128)S(1)} copy(f32[175,1024]{1,0:T(8,128)} %convolution_bitcast_fusion.2) | data formatting | bytes 1433600 | tf_op jit(solution)/shard_map/dot_general | solution.py:53
  42.7 0.0 copy-start.11
  42.7 0.0 all-to-all-done
  42.7 0.6 fusion.32
  44.1 0.1 fusion.30
  44.3 0.7 copy.48
  45.0 4.5 %all-to-all-start.1 = ((bf16[75,4,128]{2,0,1:T(8,128)(2,1)}), bf16[75,4,128]{2,0,1:T(8,128)(2,1)S(1)}, u32[]{:S(2)}, u32[]{:S(2)}) async-start(bf16[75,4,128]{2,0,1:T(8,128)(2,1)} %copy.48), calls=%async_computation.1 | async-start | bytes 163840 | tf_op jit(solution)/shard_map/all_to_all | solution.py:119
  49.4 0.0 collective-permute-done
  49.4 0.0 collective-permute-done.1
  49.4 1.4 %maximum_convert_fusion = f32[75,2,512]{2,1,0:T(2,128)S(1)} fusion(bf16[75,1,512]{2,1,0:T(2,128)(2,1)} %collective-permute-done.1, bf16[75,1,512]{2,1,0:T(2,128)(2,1)} %collective-permute-done), kind=kLoop, calls=%fused_computation.43 | loop fusion | flops 307200 | bytes 460800 | tf_op jit(solution)/shard_map/convert_element_type | solution.py:74
  50.8 0.1 pad.4
  50.9 0.1 copy.56
  51.0 0.1 fusion.22
  51.2 0.9 %broadcast_select_fusion = bf16[4,75,1024]{2,1,0:T(8,128)(2,1)} fusion(pred[4,1024]{1,0:T(4,128)(4,1)S(1)} %iota_compare_fusion.4, bf16[75,1024]{1,0:T(8,128)(2,1)S(1)} %fusion.22), kind=kLoop, calls=%fused_computation.22 | loop fusion | flops 307200 | bytes 772096 | tf_op jit(solution)/shard_map/jit(_where)/select_n | solution.py:82
  52.1 2.1 %select_n.58 = bf16[300,1024]{1,0:T(8,128)(2,1)} reshape(bf16[4,75,1024]{2,1,0:T(8,128)(2,1)} %broadcast_select_fusion) | data formatting | bytes 1228800 | tf_op jit(solution)/shard_map/jit(_where)/select_n | solution.py:82
  54.2 2.6 %fusion.45 = f32[1024,175]{1,0:T(8,128)} fusion(bf16[300,1024]{1,0:T(8,128)(2,1)} %select_n.58, bf16[175,300]{1,0:T(8,128)(2,1)} %param.19), kind=kOutput, calls=%fused_computation.84 | convolution fusion | flops 107520000 | bytes 1436200 | tf_op jit(solution)/shard_map/dot_general | solution.py:85
  56.7 6.9 %scatter_fusion = f32[175,1024]{0,1:T(8,128)S(1)} fusion(f32[175,1024]{0,1:T(8,128)S(1)} %copy.41, s32[1024]{0:T(1024)S(1)} %get-tuple-element.9, f32[1024,175]{1,0:T(8,128)} %fusion.45), kind=kCustom, calls=%fused_computation.2 | custom fusion | flops 179200 | bytes 2154496 | tf_op jit(solution)/shard_map/scatter-add | solution.py:86
  63.7 0.9 %fusion.3 = bf16[175,1024]{0,1:T(8,128)(2,1)} fusion(bf16[175,1024]{0,1:T(8,128)(2,1)S(1)} %copy.39, f32[175,1024]{0,1:T(8,128)S(1)} %scatter_fusion), kind=kLoop, calls=%fused_computation.18 | loop fusion | flops 716800 | bytes 1433600 | tf_op jit(solution)/shard_map/convert_element_type | solution.py:87
  64.6 2.0 %copy.52 = bf16[175,1024]{1,0:T(8,128)(2,1)} copy(bf16[175,1024]{0,1:T(8,128)(2,1)} %fusion.3) | data formatting | bytes 716800
  66.6 0.0 all-to-all-done.1
  66.7 2.4 %fusion.2 = f32[512,375]{1,0:T(8,128)} fusion(bf16[375,75]{0,1:T(8,128)(2,1)} %param.21, bf16[75,512]{1,0:T(8,128)(2,1)S(1)} %bitcast.56, s32[512]{0:T(512)S(1)} %bitcast.61), kind=kOutput, calls=%fused_computation.17 | convolution fusion | flops 68422144 | bytes 903098 | tf_op jit(solution)/shard_map/dot_general | solution.py:128
  69.1 4.9 %scatter_fusion.1 = f32[375,1024]{0,1:T(8,128)S(1)} fusion(f32[375,1024]{0,1:T(8,128)S(1)} %copy.50, s32[512]{0:T(512)S(1)} %compare_select_fusion.1, f32[512,375]{1,0:T(8,128)} %fusion.2), kind=kCustom, calls=%fused_computation.3 | custom fusion | flops 192000 | bytes 2306048 | tf_op jit(solution)/shard_map/scatter-add | solution.py:129
  74.0 1.1 %fusion = bf16[375,1024]{0,1:T(8,128)(2,1)} fusion(bf16[375,1024]{0,1:T(8,128)(2,1)S(1)} %copy-done.2, f32[375,1024]{0,1:T(8,128)S(1)} %scatter_fusion.1), kind=kLoop, calls=%fused_computation.6 | loop fusion | flops 1536000 | bytes 3072000 | tf_op jit(solution)/shard_map/convert_element_type | solution.py:130
  75.1 2.3 %copy.53 = bf16[375,1024]{1,0:T(8,128)(2,1)} copy(bf16[375,1024]{0,1:T(8,128)(2,1)} %fusion) | data formatting | bytes 1536000
  (31 shorter events, 0.2 us)
Async XLA Ops:
  0.6 34.7 %copy-start = (bf16[375,375]{1,0:T(8,128)(2,1)S(1)}, bf16[375,375]{1,0:T(8,128)(2,1)}, u32[]{:S(2)}) copy-start(bf16[375,375]{1,0:T(8,128)(2,1)} %param.17) | copy-start | bytes 843754
  0.6 5.4 %copy-start.8 = (s32[512,1]{0,1:T(1,128)S(1)}, s32[512,1]{0,1:T(1,128)}, u32[]{:S(2)}) copy-start(s32[512,1]{0,1:T(1,128)} %param.26) | copy-start | bytes 6148
  3.6 31.8 %copy-start.1 = (bf16[375,1024]{0,1:T(8,128)(2,1)}, bf16[375,1024]{0,1:T(8,128)(2,1)S(1)}, u32[]{:S(2)}) copy-start(bf16[375,1024]{0,1:T(8,128)(2,1)S(1)} %copy.43) | copy-start | bytes 2304004
  6.0 2.0 %copy-start.13 = (bf16[75,375]{1,0:T(8,128)(2,1)S(1)}, bf16[75,375]{1,0:T(8,128)(2,1)}, u32[]{:S(2)}) copy-start(bf16[75,375]{1,0:T(8,128)(2,1)} %param.20) | copy-start | bytes 168754
  8.0 6.1 %copy-start.9 = (s32[1024]{0:T(1024)S(1)}, s32[1024]{0:T(1024)}, u32[]{:S(2)}) copy-start(s32[1024]{0:T(1024)} %param.22) | copy-start | bytes 12292
  8.0 6.1 %copy-start.5 = (bf16[175,1024]{1,0:T(8,128)(2,1)S(1)}, bf16[175,1024]{1,0:T(8,128)(2,1)}, u32[]{:S(2)}) copy-start(bf16[175,1024]{1,0:T(8,128)(2,1)} %param.14) | copy-start | bytes 1075204
  9.3 33.5 %all-to-all-start = ((bf16[75,4,128]{2,0,1:T(8,128)(2,1)}), bf16[75,4,128]{2,0,1:T(8,128)(2,1)S(1)}, u32[]{:S(2)}, u32[]{:S(2)}) async-start(bf16[75,4,128]{2,0,1:T(8,128)(2,1)} %copy.45), calls=%async_computation | async-start | bytes 163840 | tf_op jit(solution)/shard_map/all_to_all | solution.py:107
  14.4 4.0 %copy-start.6 = (bf16[300,175]{0,1:T(8,128)(2,1)S(1)}, bf16[300,175]{0,1:T(8,128)(2,1)}, u32[]{:S(2)}) copy-start(bf16[300,175]{0,1:T(8,128)(2,1)} %param.18) | copy-start | bytes 315004
  21.5 15.7 %copy-start.3 = (bf16[75,1024]{1,0:T(8,128)(2,1)}, bf16[75,1024]{1,0:T(8,128)(2,1)S(1)}, u32[]{:S(2)}) copy-start(bf16[75,1024]{1,0:T(8,128)(2,1)S(1)} %select_reduce_fusion) | copy-start | bytes 460804
  21.6 15.6 %copy-start.12 = (s32[1,2]{1,0:T(1,128)S(1)}, s32[1,2]{1,0:T(1,128)}, u32[]{:S(2)}) copy-start(s32[1,2]{1,0:T(1,128)} %param.23) | copy-start | bytes 28
  21.6 15.7 %copy-start.7 = (bf16[175,175]{1,0:T(8,128)(2,1)S(1)}, bf16[175,175]{1,0:T(8,128)(2,1)}, u32[]{:S(2)}) copy-start(bf16[175,175]{1,0:T(8,128)(2,1)} %param.16) | copy-start | bytes 183754
  22.5 26.9 %collective-permute-start = (bf16[75,1,512]{2,1,0:T(2,128)(2,1)}, bf16[75,1,512]{2,1,0:T(2,128)(2,1)}, u32[]{:S(2)}, u32[]{:S(2)}) collective-permute-start(bf16[75,1,512]{2,1,0:T(2,128)(2,1)} %get-tuple-element.10), channel_id=1, source_target_pairs={{0,4},{4,8},{8,12},{12,16},{16,20},{20,24},{24,28},{28,32},{32,36}... | collective-permute-start | bytes 230408 | tf_op jit(solution)/shard_map/ppermute | solution.py:20
  26.6 22.9 %collective-permute-start.1 = (bf16[75,1,512]{2,1,0:T(2,128)(2,1)}, bf16[75,1,512]{2,1,0:T(2,128)(2,1)}, u32[]{:S(2)}, u32[]{:S(2)}) collective-permute-start(bf16[75,1,512]{2,1,0:T(2,128)(2,1)} %get-tuple-element.11), channel_id=1, source_target_pairs={{4,0},{8,4},{12,8},{16,12},{20,16},{24,20},{28,24},{32,28},{36,32}... | collective-permute-start | bytes 230408 | tf_op jit(solution)/shard_map/ppermute | solution.py:23
  35.4 3.8 %copy-start.10 = (f32[1024]{0:T(1024)S(1)}, f32[1024]{0:T(1024)}, u32[]{:S(2)}) copy-start(f32[1024]{0:T(1024)} %param.24) | copy-start | bytes 12292
  42.7 8.3 %copy-start.11 = (f32[1024]{0:T(1024)S(1)}, f32[1024]{0:T(1024)}, u32[]{:S(2)}) copy-start(f32[1024]{0:T(1024)} %constant.87.clone.1) | copy-start | bytes 12292
  45.0 21.6 %all-to-all-start.1 = ((bf16[75,4,128]{2,0,1:T(8,128)(2,1)}), bf16[75,4,128]{2,0,1:T(8,128)(2,1)S(1)}, u32[]{:S(2)}, u32[]{:S(2)}) async-start(bf16[75,4,128]{2,0,1:T(8,128)(2,1)} %copy.48), calls=%async_computation.1 | async-start | bytes 163840 | tf_op jit(solution)/shard_map/all_to_all | solution.py:119
  49.4 1.6 %copy-start.4 = (bf16[75,1024]{1,0:T(8,128)(2,1)S(1)}, bf16[75,1024]{1,0:T(8,128)(2,1)}, u32[]{:S(2)}) copy-start(bf16[75,1024]{1,0:T(8,128)(2,1)} %copy-done.3) | copy-start | bytes 460804
  69.1 4.9 %copy-start.2 = (bf16[375,1024]{0,1:T(8,128)(2,1)S(1)}, bf16[375,1024]{0,1:T(8,128)(2,1)}, u32[]{:S(2)}) copy-start(bf16[375,1024]{0,1:T(8,128)(2,1)} %copy-done.1) | copy-start | bytes 2304004
where the time goes:
time: 78.2 us; the launch traced here: 77.4 us
  local copies, waits for them, and re-layouts  22.5 us (29%)
  starting transfers between devices  22.1 us (28%)
  other arithmetic  21 us (27%)
  matrix products  9.99 us (13%)
  between operations  1.79 us (2%)
    ppermute x1, starting transfers between devices, extended_2(): lax.ppermute(lax.slice_in_dim(block, 0, width, axis=dim), axis, backward)  8.78 us
    scatter-add x1, other arithmetic, on_device(): tet_total = tet_div.at[:, tet_index].add(tet_lift)  6.93 us
    unnamed x36, local copies, waits for them, and re-layouts  6.23 us
    scatter-add x1, other arithmetic, on_device(): prism_total = prism_div.at[:, burn_prism].add(prism_lift)  4.93 us
    all_to_all x1, starting transfers between devices, on_device(): lax.all_to_all(outgoing, 'azim', split_axis=1, concat_axis=1, tiled=True)  4.84 us
    all_to_all x1, starting transfers between devices, on_device(): lax.all_to_all(response.reshape(face_rows, sectors, CB), 'azim', split_ax...  4.47 us
    ppermute x1, starting transfers between devices, extended_2(): lax.ppermute(lax.slice_in_dim(block, block.shape[dim] - width, None, axis...  4.04 us
    gather x1, local copies, waits for them, and re-layouts, on_device(): columns = jnp.take(tet_state, tet_index, axis=1)  3.94 us
  transfers between devices with their start and end apart: 4, of which 0 were waited for; matrix products, arithmetic and copies ran while one was open for 44% of the time, Pallas kernels for 0%

commit v1 on v0

v1 whole, which is shorter than its diff:
```python
import jax
import jax.numpy as jnp
from jax import lax
from jax.experimental import pallas as pl
from jax.experimental.pallas import tpu as pltpu
from jax.sharding import PartitionSpec as P

NV = 5
TFP = 15
FW = 75
FP = 80
BW_DEV = 512
SECTORS = 4
STEP = 0.25

BF = jnp.bfloat16
F32 = jnp.float32
NN = (((1,), (0,)), ((), ()))
NT = (((1,), (1,)), ((), ()))
TN = (((0,), (0,)), ((), ()))


def mm(a, b, dims=NN):
    return lax.dot_general(a, b, dims, preferred_element_type=F32)


def rows_of(shape):
    return lax.broadcasted_iota(jnp.int32, shape, 0)


def cols_of(shape):
    return lax.broadcasted_iota(jnp.int32, shape, 1)


def hot(mask):
    return jnp.where(mask, 1.0, 0.0).astype(BF)


def spread(rows, cols):
    r = rows_of((rows, cols))
    f = (r >= FP).astype(jnp.int32) + (r >= 2 * FP).astype(jnp.int32) + (r >= 3 * FP).astype(jnp.int32)
    c = cols_of((rows, cols))
    return hot((c == r - (FP - FW) * f) & (r - FP * f < FW))


def square_half(values):
    wide = values.astype(F32)
    return (0.5 * wide * wide).astype(BF)


def tet_left(code_ref, tet_ref, extrap_ref, low_ref, up_ref):
    pad = mm(spread(4 * FP, 4 * FW), extrap_ref[...], NT).astype(BF)
    state = tet_ref[...]
    elements = state.shape[1]
    capacity = low_ref.shape[1]
    for side, out in ((0, low_ref), (1, up_ref)):
        code = code_ref[:, side * capacity : (side + 1) * capacity]
        pick = hot(rows_of((elements, capacity)) == (code >> 2))
        columns = mm(state, pick).astype(BF)
        wide = mm(pad, columns)
        face = code & 3
        left = jnp.where(
            face < 2,
            jnp.where(face == 0, wide[:FP], wide[FP : 2 * FP]),
            jnp.where(face == 2, wide[2 * FP : 3 * FP], wide[3 * FP :]),
        )
        out[...] = left.astype(BF)


def wall_sum(prism_ref, extrap_ref, burn_ref, owner_ref, part_ref, hot_ref):
    rows = mm(extrap_ref[(NV - 1) * TFP : NV * TFP, :], prism_ref[...]).astype(BF).astype(F32)
    sums = jnp.sum(rows * rows, axis=0, keepdims=True)
    walls = burn_ref.shape[1]
    elements = prism_ref.shape[1]
    place = hot(rows_of((elements, walls)) == burn_ref[...])
    owned = hot(rows_of((8, walls)) == owner_ref[...])
    owned = mm(owned, place, NT)
    hot_ref[...] = owned
    part = jnp.sum(owned * sums, axis=1, keepdims=True)
    part_ref[...] = jnp.broadcast_to(part[None], part_ref.shape)


def tet_finish(
    count_ref, code_ref, area_ref, low_ref, up_ref, from_low_ref, from_up_ref, tet_ref, volume_ref, lift_ref, out_ref
):
    capacity = low_ref.shape[1]
    state = tet_ref[...]
    elements = state.shape[1]
    slot = cols_of((1, capacity))
    total = mm(volume_ref[...], square_half(state))
    pad = mm(lift_ref[...], spread(4 * FP, 4 * FW), NT).astype(BF)
    placed = None
    for side, own, other, normal in ((0, low_ref, from_low_ref, -1.0), (1, up_ref, from_up_ref, 1.0)):
        code = code_ref[:, side * capacity : (side + 1) * capacity]
        area = area_ref[:, side * capacity : (side + 1) * capacity]
        live = jnp.where(slot < count_ref[0, side], area, 0.0)
        left = own[...].astype(F32)
        right = other[...].astype(F32)
        speed = jnp.maximum(jnp.abs(left), jnp.abs(right))
        flux = (0.25 * normal) * (right * right - left * left) - 0.5 * speed * (right - left)
        jump = (live * flux).astype(BF)
        face = code & 3
        masked = jnp.concatenate([jnp.where(face == f, jump, jnp.zeros_like(jump)) for f in range(4)], axis=0)
        pick = hot(rows_of((elements, capacity)) == (code >> 2))
        piece = mm(masked, pick, NT)
        placed = piece if placed is None else placed + piece
    total = total + mm(pad, placed.astype(BF))
    out_ref[...] = (state.astype(F32) - STEP * total).astype(BF)


def prism_finish(parts_ref, law_ref, hot_ref, prism_ref, volume_ref, extrap_ref, lift_ref, out_ref):
    state = prism_ref[...]
    total = mm(volume_ref[...], square_half(state))
    sums = jnp.sum(parts_ref[...], axis=0)[:SECTORS]
    coef = law_ref[0, :, 0:1]
    damping = 1.0 / (1.0 + coef * sums / (BW_DEV * TFP))
    scale = coef * damping
    rows = mm(extrap_ref[...], state).astype(BF).astype(F32)
    elements = state.shape[1]
    pressure = rows[(NV - 1) * TFP :]
    squares = jnp.concatenate([pressure * pressure] * NV, axis=0)
    v = rows_of((FW, 128)) // TFP
    weight = jnp.zeros((FW, elements), F32)
    any_owner = jnp.zeros((1, elements), F32)
    for o in range(SECTORS):
        column = jnp.zeros((FW, 128), F32)
        for k in range(NV):
            gain = law_ref[0, o : o + 1, 1 + k : 2 + k] * scale[o : o + 1]
            column = jnp.where(v == k, gain, column)
        column = jnp.concatenate([column] * (elements // 128), axis=1)
        owned = hot_ref[o : o + 1, :]
        any_owner = any_owner + owned
        weight = jnp.where(owned > 0.5, column, weight)
    jump = jnp.where(any_owner > 0.5, weight * squares - rows, 0.0).astype(BF)
    total = total + mm(lift_ref[...], jump, TN)
    out_ref[...] = (state.astype(F32) - STEP * total).astype(BF)


def whole(count):
    return [pl.BlockSpec(memory_space=pltpu.VMEM)] * count


def call(kernel, name, out_shape, flops, moved, specs, *args):
    single = not isinstance(out_shape, tuple)
    return pl.pallas_call(
        kernel,
        out_shape=out_shape,
        in_specs=specs,
        out_specs=whole(1)[0] if single else tuple(whole(len(out_shape))),
        cost_estimate=pl.CostEstimate(flops=flops, bytes_accessed=moved, transcendentals=0),
        compiler_params=pltpu.CompilerParams(vmem_limit_bytes=40 * 1024 * 1024),
        name=name,
    )(*args)


def on_device(
    tet_state,
    prism_state,
    tet_volume,
    prism_volume,
    face_extrap,
    face_lift,
    wall_extrap,
    wall_lift,
    face_code,
    face_count,
    face_area,
    burn_prism,
    burn_owner,
    burn_law,
):
    slots = face_code.shape[0]
    capacity = slots // 2
    code = face_code.reshape(1, slots)
    area = face_area.reshape(1, slots)
    burn = burn_prism.reshape(1, -1)
    owner = burn_owner.reshape(1, -1)
    side = jax.ShapeDtypeStruct((FP, capacity), BF)
    low, up = call(
        tet_left, "tet_left", (side, side), 500_000_000, 600_000, whole(3), code, tet_state, face_extrap.T
    )
    count = lax.axis_size("axial")
    forward = [(i, i + 1) for i in range(count - 1)]
    backward = [(j, i) for i, j in forward]
    from_low = lax.ppermute(up, "axial", forward)
    from_up = lax.ppermute(low, "axial", backward)
    part, owned = call(
        wall_sum,
        "wall_sum",
        (
            jax.ShapeDtypeStruct((SECTORS, 8, 128), F32),
            jax.ShapeDtypeStruct((8, prism_state.shape[1]), F32),
        ),
        100_000_000,
        900_000,
        whole(4),
        prism_state,
        wall_extrap,
        burn,
        owner,
    )
    parts = lax.all_to_all(part, "azim", split_axis=0, concat_axis=0, tiled=True)
    tet_new = call(
        tet_finish,
        "tet_finish",
        jax.ShapeDtypeStruct(tet_state.shape, BF),
        800_000_000,
        1_500_000,
        [pl.BlockSpec(memory_space=pltpu.SMEM)] + whole(9),
        face_count,
        code,
        area,
        low,
        up,
        from_low,
        from_up,
        tet_state,
        tet_volume,
        face_lift,
    )
    prism_new = call(
        prism_finish,
        "prism_finish",
        jax.ShapeDtypeStruct(prism_state.shape, BF),
        400_000_000,
        2_000_000,
        whole(7),
        parts,
        burn_law,
        owned,
        prism_state,
        prism_volume,
        wall_extrap,
        wall_lift.T,
    )
    return (tet_new, prism_new)


def solution(mesh):
    elements = P(None, ("axial", "azim"))
    placed = (
        elements,
        elements,
        P(),
        P(),
        P(),
        P(),
        P(),
        P(),
        P(("axial", "azim")),
        P(("axial", "azim"), None),
        P(("axial", "azim")),
        P(("axial", "azim")),
        P(("axial", "azim"), None),
        P("axial", None, None),
    )
    return jax.shard_map(
        on_device, mesh=mesh, in_specs=placed, out_specs=(elements, elements), check_vma=False
    )
```

time: 78.2 us -> 32.2 us (0.41)
  other arithmetic: 21 us -> 0 us
  local copies, waits for them, and re-layouts: 22.5 us -> 3.9 us
  matrix products: 9.99 us -> 0 us
  starting transfers between devices: 22.1 us -> 14.3 us
  blocking collectives: 0 us -> 6.55 us
  Pallas kernels: 0 us -> 6.26 us
  between operations: 1.79 us -> 0.79 us
    scatter-add x2 -> x0, other arithmetic: 11.9 us -> none  [the longest x1 6.93 us: on_device(): tet_total = tet_div.at[:, tet_index].add(tet_lift)]
    dot_general x6 -> x0, matrix products: 9.99 us -> none  [the longest x1 2.55 us: on_device(): tet_lift = jnp.dot(face_lift, placed, preferred_element_type=jnp.float32)]
    all_to_all x2 -> x0, starting transfers between devices: 9.32 us -> none  [the longest x1 4.84 us: on_device(): lax.all_to_all(outgoing, 'azim', split_axis=1, concat_axis=1, tiled=True)]
    all_to_all x0 -> x1, blocking collectives: none -> 6.55 us  [on_device(): lax.all_to_all(part, 'azim', split_axis=0, concat_axis=0, tiled=True)]
    pallas_call x0 -> x4, Pallas kernels: none -> 6.26 us  [call(): pl.pallas_call(kernel, out_shape=out_shape, in_specs=specs, out_specs=who...]
    gather x2 -> x0, local copies, waits for them, and re-layouts: 5.88 us -> none  [the longest x1 3.94 us: on_device(): columns = jnp.take(tet_state, tet_index, axis=1)]
    convert_element_type x6 -> x0, other arithmetic: 4.43 us -> none  [the longest x1 1.38 us: on_device(): right_wide = right_rows.astype(jnp.float32)]
    dot_general x2 -> x0, local copies, waits for them, and re-layouts: 3.3 us -> none  [the longest x1 1.86 us: on_device(): jnp.dot(prism_volume, square_half(prism_state), preferred_element_type=jn...]
  transfers between devices with their start and end apart: 4 -> 2, of which waited for: 0 -> 0; matrix products, arithmetic and copies ran while one was open for 44% -> 0% of each run, Pallas kernels for 0% -> 8%
where the time goes in v1:
time: 32.2 us; the launch traced here: 31.9 us
  starting transfers between devices  14.3 us (44%)
  blocking collectives  6.55 us (20%)
  Pallas kernels  6.26 us (19%)
  local copies, waits for them, and re-layouts  3.9 us (12%)
  between operations  0.79 us (2%)
    ppermute x1, starting transfers between devices, on_device(): from_up = lax.ppermute(low, 'axial', backward)  12.4 us
    all_to_all x1, blocking collectives, on_device(): lax.all_to_all(part, 'azim', split_axis=0, concat_axis=0, tiled=True)  6.55 us
    pallas_call x4, Pallas kernels, call(): pl.pallas_call(kernel, out_shape=out_shape, in_specs=specs, out_specs=who...  6.26 us
    unnamed x32, local copies, waits for them, and re-layouts  3.9 us
    ppermute x1, starting transfers between devices, on_device(): from_low = lax.ppermute(up, 'axial', forward)  1.92 us
  transfers between devices with their start and end apart: 2, of which 0 were waited for; matrix products, arithmetic and copies ran while one was open for 0% of the time, Pallas kernels for 8%

profile of v1, /device:TPU:1, one launch (start us, length us, event | category | flops | bytes accessed | tf_op | source)
XLA Modules:
  0.0 31.9 jit_solution(16600889903698558719)
XLA Ops:
  0.6 0.0 copy-start.7
  0.6 1.0 %copy-done.7 = bf16[175,1024]{1,0:T(8,128)(2,1)S(1)} copy-done((bf16[175,1024]{1,0:T(8,128)(2,1)S(1)}, bf16[175,1024]{1,0:T(8,128)(2,1)}, u32[]{:S(2)}) %copy-start.7) | copy-done | bytes 358424
  1.6 0.0 copy-start.9
  1.6 0.9 %copy-done.9 = bf16[300,175]{0,1:T(8,128)(2,1)S(1)} copy-done((bf16[300,175]{0,1:T(8,128)(2,1)S(1)}, bf16[300,175]{0,1:T(8,128)(2,1)}, u32[]{:S(2)}) %copy-start.9) | copy-done | bytes 105024
  2.5 0.0 copy-start.12
  2.5 0.7 %copy-done.12 = s32[1024]{0:T(1024)S(1)} copy-done((s32[1024]{0:T(1024)S(1)}, s32[1024]{0:T(1024)}, u32[]{:S(2)}) %copy-start.12) | copy-done | bytes 4120
  3.2 0.0 copy-start
  3.2 0.0 copy-start.2
  3.2 1.2 %tet_left.1 = (bf16[80,512]{1,0:T(8,128)(2,1)S(1)}, bf16[80,512]{1,0:T(8,128)(2,1)S(1)}) custom-call(s32[1,1024]{1,0:T(1,128)S(1)} %bitcast.10, bf16[175,1024]{1,0:T(8,128)(2,1)S(1)} %copy-done.7, bf16[175,300]{1,0:T(8,128)(2,1)S(1)} %bitcast.9), custom_call_target="tpu_custom_call" | custom-call | flops 500000000 | bytes 600000 | tf_op jit(solution)/shard_map/tet_left/pallas_call | solution.py:145
  4.4 12.4 %collective-permute-start.1 = (bf16[80,512]{1,0:T(8,128)(2,1)S(1)}, bf16[80,512]{1,0:T(8,128)(2,1)S(1)}, u32[]{:S(2)}, u32[]{:S(2)}) collective-permute-start(bf16[80,512]{1,0:T(8,128)(2,1)S(1)} %get-tuple-element.6.low_ref), channel_id=1, source_target_pairs={{4,0},{8,4},{12,8},{16,12},{20,16},{24,20},{28,24},{32,28},{36,32}... | collective-permute-start | bytes 245768 | tf_op jit(solution)/shard_map/ppermute | solution.py:186
  16.8 0.0 copy-start.5
  16.8 0.0 copy-start.4
  16.9 1.9 %collective-permute-start = (bf16[80,512]{1,0:T(8,128)(2,1)S(1)}, bf16[80,512]{1,0:T(8,128)(2,1)S(1)}, u32[]{:S(2)}, u32[]{:S(2)}) collective-permute-start(bf16[80,512]{1,0:T(8,128)(2,1)S(1)} %get-tuple-element.7.up_ref), channel_id=1, source_target_pairs={{0,4},{4,8},{8,12},{12,16},{16,20},{20,24},{24,28},{28,32},{32,36}... | collective-permute-start | bytes 245768 | tf_op jit(solution)/shard_map/ppermute | solution.py:185
  18.8 0.0 copy-done
  18.8 0.0 copy-done.2
  18.8 0.0 copy-done.5
  18.8 0.0 copy-done.4
  18.8 0.0 copy-start.1
  18.8 0.0 copy-start.3
  18.8 0.6 %wall_sum.1 = (f32[4,8,128]{2,1,0:T(8,128)S(1)}, f32[8,1024]{1,0:T(8,128)S(1)}) custom-call(bf16[375,1024]{1,0:T(8,128)(2,1)S(1)} %copy-done, bf16[75,375]{1,0:T(8,128)(2,1)S(1)} %copy-done.2, s32[1,512]{1,0:T(1,128)S(1)} %bitcast.7, s32[1,512]{1,0:T(1,128)S(1)} %bitcast.8), custom_call_target="tpu_custom_call" | custom-call | flops 100000000 | bytes 900000 | tf_op jit(solution)/shard_map/wall_sum/pallas_call | solution.py:145
  19.4 6.6 %all_to_all.5.parts_ref = f32[4,8,128]{2,1,0:T(8,128)S(1)} all-to-all(f32[4,8,128]{2,1,0:T(8,128)S(1)} %get-tuple-element.8), channel_id=1, replica_groups=mesh['axial'=192,'azim'=4] {'azim'}, dimensions={0} | all-to-all | bytes 32768 | tf_op jit(solution)/shard_map/all_to_all | solution.py:202
  26.0 0.0 copy-start.6
  26.0 0.0 copy-done.1
  26.0 0.0 copy-done.3
  26.0 0.7 %copy-done.6 = f32[1,4,6]{2,1,0:T(4,128)S(1)} copy-done((f32[1,4,6]{2,1,0:T(4,128)S(1)}, f32[1,4,6]{2,1,0:T(4,128)}, u32[]{:S(2)}) %copy-start.6) | copy-done | bytes 120
  26.6 0.0 copy-start.8
  26.7 0.0 copy-start.10
  26.7 0.0 copy-start.11
  26.7 0.0 copy-start.13
  26.7 0.0 copy-start.14
  26.7 1.9 %prism_finish.1 = bf16[375,1024]{1,0:T(8,128)(2,1)} custom-call(f32[4,8,128]{2,1,0:T(8,128)S(1)} %all_to_all.5.parts_ref, f32[1,4,6]{2,1,0:T(4,128)S(1)} %copy-done.6, f32[8,1024]{1,0:T(8,128)S(1)} %get-tuple-element.9.hot_ref, bf16[375,1024]{1,0:T(8,128)(2,1)S(1)} %copy-done, bf16[375,375]{1,0:T(8,128)(2,1)S(1)} %copy-done.1, ...), custom_call_target="tpu_custom_call" | custom-call | flops 400000000 | bytes 2000000 | tf_op jit(solution)/shard_map/prism_finish/pallas_call | solution.py:145
  28.6 0.0 copy-start.15
  28.6 0.0 collective-permute-done.1.from_up_ref
  28.6 0.0 collective-permute-done.from_low_ref
  28.6 0.0 copy-done.8
  28.6 0.0 copy-done.10
  28.6 0.0 copy-done.11
  28.7 0.0 copy-done.13
  28.7 0.0 copy-done.14
  28.7 0.6 %copy-done.15 = s32[1,2]{1,0:T(1,128)S(1)} copy-done((s32[1,2]{1,0:T(1,128)S(1)}, s32[1,2]{1,0:T(1,128)}, u32[]{:S(2)}) %copy-start.15) | copy-done | bytes 32
  29.3 2.6 %tet_finish.1 = bf16[175,1024]{1,0:T(8,128)(2,1)} custom-call(s32[1,2]{1,0:T(1,128)S(1)} %copy-done.15, s32[1,1024]{1,0:T(1,128)S(1)} %bitcast.11, f32[1,1024]{1,0:T(1,128)S(1)} %bitcast.12, bf16[80,512]{1,0:T(8,128)(2,1)S(1)} %get-tuple-element.6.low_ref, bf16[80,512]{1,0:T(8,128)(2,1)S(1)} %get-tuple-element.7.up_ref, ...), custom_call_target="tpu_custom_call" | custom-call | flops 800000000 | bytes 1500000 | tf_op jit(solution)/shard_map/tet_finish/pallas_call | solution.py:145
Async XLA Ops:
  0.6 1.0 %copy-start.7 = (bf16[175,1024]{1,0:T(8,128)(2,1)S(1)}, bf16[175,1024]{1,0:T(8,128)(2,1)}, u32[]{:S(2)}) copy-start(bf16[175,1024]{1,0:T(8,128)(2,1)} %tet_ref.3) | copy-start | bytes 1075204
  1.6 0.9 %copy-start.9 = (bf16[300,175]{0,1:T(8,128)(2,1)S(1)}, bf16[300,175]{0,1:T(8,128)(2,1)}, u32[]{:S(2)}) copy-start(bf16[300,175]{0,1:T(8,128)(2,1)} %param.18) | copy-start | bytes 315004
  2.5 0.7 %copy-start.12 = (s32[1024]{0:T(1024)S(1)}, s32[1024]{0:T(1024)}, u32[]{:S(2)}) copy-start(s32[1024]{0:T(1024)} %param.22) | copy-start | bytes 12292
  3.2 15.6 %copy-start = (bf16[375,1024]{1,0:T(8,128)(2,1)S(1)}, bf16[375,1024]{1,0:T(8,128)(2,1)}, u32[]{:S(2)}) copy-start(bf16[375,1024]{1,0:T(8,128)(2,1)} %prism_ref.3) | copy-start | bytes 2304004
  3.2 15.6 %copy-start.2 = (bf16[75,375]{1,0:T(8,128)(2,1)S(1)}, bf16[75,375]{1,0:T(8,128)(2,1)}, u32[]{:S(2)}) copy-start(bf16[75,375]{1,0:T(8,128)(2,1)} %extrap_ref.3) | copy-start | bytes 168754
  4.4 24.2 %collective-permute-start.1 = (bf16[80,512]{1,0:T(8,128)(2,1)S(1)}, bf16[80,512]{1,0:T(8,128)(2,1)S(1)}, u32[]{:S(2)}, u32[]{:S(2)}) collective-permute-start(bf16[80,512]{1,0:T(8,128)(2,1)S(1)} %get-tuple-element.6.low_ref), channel_id=1, source_target_pairs={{4,0},{8,4},{12,8},{16,12},{20,16},{24,20},{28,24},{32,28},{36,32}... | collective-permute-start | bytes 245768 | tf_op jit(solution)/shard_map/ppermute | solution.py:186
  16.8 2.0 %copy-start.5 = (s32[512,1]{0,1:T(1,128)S(1)}, s32[512,1]{0,1:T(1,128)}, u32[]{:S(2)}) copy-start(s32[512,1]{0,1:T(1,128)} %param.26) | copy-start | bytes 6148
  16.8 2.0 %copy-start.4 = (s32[512]{0:T(512)S(1)}, s32[512]{0:T(512)}, u32[]{:S(2)}) copy-start(s32[512]{0:T(512)} %param.25) | copy-start | bytes 6148
  16.9 11.8 %collective-permute-start = (bf16[80,512]{1,0:T(8,128)(2,1)S(1)}, bf16[80,512]{1,0:T(8,128)(2,1)S(1)}, u32[]{:S(2)}, u32[]{:S(2)}) collective-permute-start(bf16[80,512]{1,0:T(8,128)(2,1)S(1)} %get-tuple-element.7.up_ref), channel_id=1, source_target_pairs={{0,4},{4,8},{8,12},{12,16},{16,20},{20,24},{24,28},{28,32},{32,36}... | collective-permute-start | bytes 245768 | tf_op jit(solution)/shard_map/ppermute | solution.py:185
  18.8 7.2 %copy-start.1 = (bf16[375,375]{1,0:T(8,128)(2,1)S(1)}, bf16[375,375]{1,0:T(8,128)(2,1)}, u32[]{:S(2)}) copy-start(bf16[375,375]{1,0:T(8,128)(2,1)} %volume_ref.3) | copy-start | bytes 843754
  18.8 7.1 %copy-start.3 = (bf16[375,75]{0,1:T(8,128)(2,1)S(1)}, bf16[375,75]{0,1:T(8,128)(2,1)}, u32[]{:S(2)}) copy-start(bf16[375,75]{0,1:T(8,128)(2,1)} %param.21) | copy-start | bytes 168754
  26.0 0.7 %copy-start.6 = (f32[1,4,6]{2,1,0:T(4,128)S(1)}, f32[1,4,6]{2,1,0:T(4,128)}, u32[]{:S(2)}) copy-start(f32[1,4,6]{2,1,0:T(4,128)} %law_ref.1) | copy-start | bytes 292
  26.6 2.0 %copy-start.8 = (bf16[175,1024]{1,0:T(8,128)(2,1)S(1)}, bf16[175,1024]{1,0:T(8,128)(2,1)}, u32[]{:S(2)}) copy-start(bf16[175,1024]{1,0:T(8,128)(2,1)} %tet_ref.3) | copy-start | bytes 1075204
  26.7 2.0 %copy-start.10 = (bf16[175,300]{1,0:T(8,128)(2,1)S(1)}, bf16[175,300]{1,0:T(8,128)(2,1)}, u32[]{:S(2)}) copy-start(bf16[175,300]{1,0:T(8,128)(2,1)} %lift_ref.1) | copy-start | bytes 315004
  26.7 2.0 %copy-start.11 = (bf16[175,175]{1,0:T(8,128)(2,1)S(1)}, bf16[175,175]{1,0:T(8,128)(2,1)}, u32[]{:S(2)}) copy-start(bf16[175,175]{1,0:T(8,128)(2,1)} %volume_ref.2) | copy-start | bytes 183754
  26.7 2.0 %copy-start.13 = (s32[1024]{0:T(1024)S(1)}, s32[1024]{0:T(1024)}, u32[]{:S(2)}) copy-start(s32[1024]{0:T(1024)} %param.22) | copy-start | bytes 12292
  26.7 2.0 %copy-start.14 = (f32[1024]{0:T(1024)S(1)}, f32[1024]{0:T(1024)}, u32[]{:S(2)}) copy-start(f32[1024]{0:T(1024)} %param.24) | copy-start | bytes 12292
  28.6 0.7 %copy-start.15 = (s32[1,2]{1,0:T(1,128)S(1)}, s32[1,2]{1,0:T(1,128)}, u32[]{:S(2)}) copy-start(s32[1,2]{1,0:T(1,128)} %count_ref.1) | copy-start | bytes 28

commit v2 on v1

v2 whole, which is shorter than its diff:
```python
import jax
import jax.numpy as jnp
from jax import lax
from jax.experimental import pallas as pl
from jax.experimental.pallas import tpu as pltpu
from jax.sharding import PartitionSpec as P

NV = 5
TFP = 15
FW = 75
FP = 80
BW_DEV = 512
SECTORS = 4
STEP = 0.25

BF = jnp.bfloat16
F32 = jnp.float32
NN = (((1,), (0,)), ((), ()))
NT = (((1,), (1,)), ((), ()))
TN = (((0,), (0,)), ((), ()))


def mm(a, b, dims=NN):
    return lax.dot_general(a, b, dims, preferred_element_type=F32)


def rows_of(shape):
    return lax.broadcasted_iota(jnp.int32, shape, 0)


def cols_of(shape):
    return lax.broadcasted_iota(jnp.int32, shape, 1)


def hot(mask):
    return jnp.where(mask, 1.0, 0.0).astype(BF)


def spread(rows, cols):
    r = rows_of((rows, cols))
    f = (r >= FP).astype(jnp.int32) + (r >= 2 * FP).astype(jnp.int32) + (r >= 3 * FP).astype(jnp.int32)
    c = cols_of((rows, cols))
    return hot((c == r - (FP - FW) * f) & (r - FP * f < FW))


def square_half(values):
    wide = values.astype(F32)
    return (0.5 * wide * wide).astype(BF)


def faces_of(code, state, pad):
    pick = hot(rows_of((state.shape[1], code.shape[1])) == (code >> 2))
    wide = mm(pad, mm(state, pick).astype(BF))
    face = code & 3
    return jnp.where(
        face < 2,
        jnp.where(face == 0, wide[:FP], wide[FP : 2 * FP]),
        jnp.where(face == 2, wide[2 * FP : 3 * FP], wide[3 * FP :]),
    ).astype(BF)


def load_kernel(*refs):
    loads, refs = refs[:14], refs[14:]
    (part_ref, pad_ref, owned_ref, live_ref), refs = refs[:4], refs[4:]
    (code_ref, tet_ref, prism_ref, volume_ref, prism_volume_ref, lift_ref, wall_lift_ref, wall_ref, law_ref), refs = refs[:9], refs[9:]
    burn_ref, owner_ref, extrap_ref, count_ref, area_ref, sems = refs
    targets = (
        burn_ref, owner_ref, wall_ref, extrap_ref, prism_ref, code_ref, tet_ref,
        count_ref, area_ref, law_ref, volume_ref, prism_volume_ref, lift_ref, wall_lift_ref,
    )
    copies = [pltpu.make_async_copy(a, b, sems.at[n]) for n, (a, b) in enumerate(zip(loads, targets))]
    for copy in copies:
        copy.start()
    for copy in copies[:4]:
        copy.wait()
    pad_ref[...] = mm(spread(4 * FP, 4 * FW), extrap_ref[...], NT).astype(BF)
    walls = burn_ref.shape[1]
    place = hot(rows_of((prism_ref.shape[1], walls)) == burn_ref[...])
    owned = mm(hot(rows_of((8, walls)) == owner_ref[...]), place, NT)
    owned_ref[...] = owned
    for copy in copies[4:]:
        copy.wait()
    rows = mm(wall_ref[(NV - 1) * TFP : NV * TFP, :], prism_ref[...]).astype(BF).astype(F32)
    sums = jnp.sum(rows * rows, axis=0, keepdims=True)
    part_ref[...] = jnp.broadcast_to(jnp.sum(owned * sums, axis=1, keepdims=True), part_ref.shape)
    capacity = live_ref.shape[1] // 2
    slot = cols_of((1, capacity))
    for side in range(2):
        area = area_ref[:, side * capacity : (side + 1) * capacity]
        live_ref[:, side * capacity : (side + 1) * capacity] = jnp.where(slot < count_ref[:, side : side + 1], area, 0.0)


def face_kernel(code_ref, tet_ref, pad_ref, low_ref, up_ref):
    capacity = low_ref.shape[1]
    state = tet_ref[...]
    pad = pad_ref[...]
    low_ref[...] = faces_of(code_ref[:, :capacity], state, pad)
    up_ref[...] = faces_of(code_ref[:, capacity:], state, pad)


def local_kernel(
    tet_ref, prism_ref, volume_ref, prism_volume_ref, wall_ref, lift_ref, law_ref, owned_ref,
    tet_part_ref, prism_part_ref, rows_ref, gain_ref, pad_ref,
):
    state = tet_ref[...]
    tet_part_ref[...] = state.astype(F32) - STEP * mm(volume_ref[...], square_half(state))
    pad_ref[...] = mm(lift_ref[...], spread(4 * FP, 4 * FW), NT).astype(BF)
    state = prism_ref[...]
    prism_part_ref[...] = state.astype(F32) - STEP * mm(prism_volume_ref[...], square_half(state))
    rows = mm(wall_ref[...], state).astype(BF).astype(F32)
    elements = rows.shape[1]
    pressure = rows[(NV - 1) * TFP :]
    squares = jnp.concatenate([pressure * pressure] * NV, axis=0)
    v = rows_of((FW, 128)) // TFP
    weight = jnp.zeros((FW, elements), F32)
    any_owner = jnp.zeros((1, elements), F32)
    for o in range(SECTORS):
        column = jnp.zeros((FW, 128), F32)
        for k in range(NV):
            gain = law_ref[0, o : o + 1, 1 + k : 2 + k] * law_ref[0, o : o + 1, 0:1]
            column = jnp.where(v == k, gain, column)
        column = jnp.concatenate([column] * (elements // 128), axis=1)
        owned = owned_ref[o : o + 1, :]
        any_owner = any_owner + owned
        weight = jnp.where(owned > 0.5, column, weight)
    gain_ref[...] = weight * squares
    rows_ref[...] = jnp.where(any_owner > 0.5, rows, 0.0)


def tet_kernel(code_ref, live_ref, low_ref, up_ref, from_low_ref, from_up_ref, part_ref, pad_ref, out_ref):
    capacity = low_ref.shape[1]
    elements = part_ref.shape[1]
    placed = None
    for side, own, other, normal in ((0, low_ref, from_low_ref, -1.0), (1, up_ref, from_up_ref, 1.0)):
        code = code_ref[:, side * capacity : (side + 1) * capacity]
        live = live_ref[:, side * capacity : (side + 1) * capacity]
        left = own[...].astype(F32)
        right = other[...].astype(F32)
        speed = jnp.maximum(jnp.abs(left), jnp.abs(right))
        flux = (0.25 * normal) * (right * right - left * left) - 0.5 * speed * (right - left)
        jump = (live * flux).astype(BF)
        face = code & 3
        masked = jnp.concatenate([jnp.where(face == f, jump, jnp.zeros_like(jump)) for f in range(4)], axis=0)
        pick = hot(rows_of((elements, capacity)) == (code >> 2))
        piece = mm(masked, pick, NT)
        placed = piece if placed is None else placed + piece
    out_ref[...] = (part_ref[...] - STEP * mm(pad_ref[...], placed.astype(BF))).astype(BF)


def prism_kernel(
    tet_ref, pair_ref, other_ref, law_ref, owned_ref, rows_ref, gain_ref, part_ref, lift_ref,
    tet_hbm, prism_hbm, prism_ref, sems,
):
    tet_out = pltpu.make_async_copy(tet_ref, tet_hbm, sems.at[0])
    tet_out.start()
    sums = (pair_ref[...] + other_ref[...])[:SECTORS]
    damping = 1.0 / (1.0 + law_ref[0, :, 0:1] * sums / (BW_DEV * TFP))
    elements = part_ref.shape[1]
    width = elements // 4
    lift = lift_ref[...]
    outs = []
    for n in range(4):
        at = slice(n * width, (n + 1) * width)
        factor = jnp.zeros((1, width), F32)
        for o in range(SECTORS):
            row = jnp.concatenate([damping[o : o + 1]] * (width // 128), axis=1)
            factor = jnp.where(owned_ref[o : o + 1, at] > 0.5, row, factor)
        jump = (gain_ref[:, at] * factor - rows_ref[:, at]).astype(BF)
        prism_ref[:, at] = (part_ref[:, at] - STEP * mm(lift, jump, TN)).astype(BF)
        out = pltpu.make_async_copy(prism_ref.at[:, at], prism_hbm.at[:, at], sems.at[1 + n])
        out.start()
        outs.append(out)
    for out in outs:
        out.wait()
    tet_out.wait()


VM = pl.BlockSpec(memory_space=pltpu.VMEM)
HB = pl.BlockSpec(memory_space=pltpu.HBM)


def call(kernel, name, outs, out_specs, specs, flops, moved, args, scratch=()):
    return pl.pallas_call(
        kernel,
        out_shape=outs,
        in_specs=specs,
        out_specs=out_specs,
        scratch_shapes=scratch,
        cost_estimate=pl.CostEstimate(flops=flops, bytes_accessed=moved, transcendentals=0),
        compiler_params=pltpu.CompilerParams(vmem_limit_bytes=32 * 1024 * 1024),
        name=name,
    )(*args)


def like(value):
    return pltpu.VMEM(value.shape, value.dtype)


def swap(value, axis, pairs):
    return lax.ppermute(value, axis, list(pairs) + [(j, i) for i, j in pairs])


def on_device(
    tet_state,
    prism_state,
    tet_volume,
    prism_volume,
    face_extrap,
    face_lift,
    wall_extrap,
    wall_lift,
    face_code,
    face_count,
    face_area,
    burn_prism,
    burn_owner,
    burn_law,
):
    slots = face_code.shape[0]
    capacity = slots // 2
    code = face_code.reshape(1, slots)
    area = face_area.reshape(1, slots)
    burn = burn_prism.reshape(1, -1)
    owner = burn_owner.reshape(1, -1)
    extrap = face_extrap.T
    wall_lift = wall_lift.T
    operands = (
        burn, owner, wall_extrap, extrap, prism_state, code, tet_state,
        face_count, area, burn_law, tet_volume, prism_volume, face_lift, wall_lift,
    )
    kept = (code, tet_state, prism_state, tet_volume, prism_volume, face_lift, wall_lift, wall_extrap, burn_law)
    side = pltpu.VMEM((FP, capacity), BF)
    outs = (
        pltpu.VMEM((8, 128), F32),
        pltpu.VMEM((4 * FP, tet_state.shape[0]), BF),
        pltpu.VMEM((8, prism_state.shape[1]), F32),
        pltpu.VMEM((1, slots), F32),
    ) + tuple(like(x) for x in kept)
    part, face_pad, owned, live, code, tet, prism, tet_vol, prism_vol, lift, wall_lift, wall, law = call(
        load_kernel,
        "load",
        outs,
        (VM,) * len(outs),
        [HB] * len(operands),
        5_000_000_000,
        3_000_000,
        tuple(pltpu.with_memory_space_constraint(x, pltpu.HBM) for x in operands),
        [like(x) for x in (burn, owner, extrap, face_count, area)]
        + [pltpu.SemaphoreType.DMA((len(operands),))],
    )
    half = swap(part, "azim", ((0, 1), (2, 3)))
    low, up = call(
        face_kernel, "faces", (side, side), (VM, VM), [VM] * 3, 5_000_000_000, 600_000, (code, tet, face_pad)
    )
    count = lax.axis_size("axial")
    forward = [(i, i + 1) for i in range(count - 1)]
    from_low = lax.ppermute(up, "axial", forward)
    from_up = lax.ppermute(low, "axial", [(j, i) for i, j in forward])
    pair = part + half
    other = swap(pair, "azim", ((1, 2), (0, 3)))
    pair, tet, prism = lax.optimization_barrier((pair, tet, prism))
    tet_part, prism_part, rows, gain, pad = call(
        local_kernel,
        "local",
        (
            pltpu.VMEM(tet.shape, F32),
            pltpu.VMEM(prism.shape, F32),
            pltpu.VMEM((FW, prism.shape[1]), F32),
            pltpu.VMEM((FW, prism.shape[1]), F32),
            pltpu.VMEM((tet.shape[0], 4 * FP), BF),
        ),
        (VM,) * 5,
        [VM] * 8,
        5_000_000_000,
        4_000_000,
        (tet, prism, tet_vol, prism_vol, wall, lift, law, owned),
    )
    tet_new = call(
        tet_kernel,
        "tet_finish",
        like(tet),
        VM,
        [VM] * 8,
        5_000_000_000,
        3_000_000,
        (code, live, low, up, from_low, from_up, tet_part, pad),
    )
    tet_new, prism_new = call(
        prism_kernel,
        "prism_finish",
        (jax.ShapeDtypeStruct(tet.shape, BF), jax.ShapeDtypeStruct(prism.shape, BF)),
        (HB, HB),
        [VM] * 9,
        5_000_000_000,
        3_000_000,
        (tet_new, pair, other, law, owned, rows, gain, prism_part, wall_lift),
        [like(prism), pltpu.SemaphoreType.DMA((5,))],
    )
    return (tet_new, prism_new)


def solution(mesh):
    elements = P(None, ("axial", "azim"))
    placed = (
        elements,
        elements,
        P(),
        P(),
        P(),
        P(),
        P(),
        P(),
        P(("axial", "azim")),
        P(("axial", "azim"), None),
        P(("axial", "azim")),
        P(("axial", "azim")),
        P(("axial", "azim"), None),
        P("axial", None, None),
    )
    return jax.shard_map(
        on_device, mesh=mesh, in_specs=placed, out_specs=(elements, elements), check_vma=False
    )
```

time: 32.2 us -> 26.6 us (0.83)
  blocking collectives: 6.55 us -> 0 us
  local copies, waits for them, and re-layouts: 3.9 us -> 0 us
  starting transfers between devices: 14.3 us -> 17.6 us
  waiting for transfers between devices: 0.01 us -> 1.56 us
    all_to_all x1 -> x0, blocking collectives: 6.55 us -> none  [on_device(): lax.all_to_all(part, 'azim', split_axis=0, concat_axis=0, tiled=True)]
    unnamed x32 -> x0, local copies, waits for them, and re-layouts: 3.9 us -> none
    ppermute x1, starting transfers between devices: 1.92 us -> 4.04 us  [on_device(): from_low = lax.ppermute(up, 'axial', forward)]
    ppermute x1 -> x3, waiting for transfers between devices: 0.01 us -> 1.56 us  [the longest x2 1.55 us: swap(): return lax.ppermute(value, axis, list(pairs) + [(j, i) for i, j in pairs])]
    ppermute x1 -> x3, starting transfers between devices: 12.4 us -> 13.5 us  [the longest x1 7.65 us: on_device(): from_up = lax.ppermute(low, 'axial', [(j, i) for i, j in forward])]
    pallas_call x4 -> x5, Pallas kernels: 6.26 us -> 6.54 us  [call(): pl.pallas_call(kernel, out_shape=outs, in_specs=specs, out_specs=out_spec...]
  transfers between devices with their start and end apart: 2 -> 4, of which waited for: 0 -> 1; matrix products, arithmetic and copies ran while one was open for 0% -> 0% of each run, Pallas kernels for 8% -> 12%
where the time goes in v2:
time: 26.6 us; the launch traced here: 26.4 us
  starting transfers between devices  17.6 us (66%)
  Pallas kernels  6.54 us (25%)
  waiting for transfers between devices  1.56 us (6%)
  between operations  0.73 us (3%)
    ppermute x1, starting transfers between devices, on_device(): from_up = lax.ppermute(low, 'axial', [(j, i) for i, j in forward])  7.65 us
    pallas_call x5, Pallas kernels, call(): pl.pallas_call(kernel, out_shape=outs, in_specs=specs, out_specs=out_spec...  6.54 us
    ppermute x2, starting transfers between devices, swap(): return lax.ppermute(value, axis, list(pairs) + [(j, i) for i, j in pairs])  5.87 us
    ppermute x1, starting transfers between devices, on_device(): from_low = lax.ppermute(up, 'axial', forward)  4.04 us
    ppermute x2, waiting for transfers between devices, swap(): return lax.ppermute(value, axis, list(pairs) + [(j, i) for i, j in pairs])  1.55 us
  transfers between devices with their start and end apart: 4, of which 1 were waited for; matrix products, arithmetic and copies ran while one was open for 0% of the time, Pallas kernels for 12%

profile of v2, /device:TPU:1, one launch (start us, length us, event | category | flops | bytes accessed | tf_op | source)
XLA Modules:
  0.0 26.4 jit_solution(4113260602797984841)
XLA Ops:
  0.6 2.0 %load.1 = (f32[8,128]{1,0:T(8,128)S(1)}, bf16[320,175]{1,0:T(8,128)(2,1)S(1)}, f32[8,1024]{1,0:T(8,128)S(1)}, f32[1,1024]{1,0:T(1,128)S(1)}, s32[1,1024]{1,0:T(1...) custom-call(s32[1,512]{1,0:T(1,128)} %bitcast.10, ...), custom_call_target="tpu_custom_call" | custom-call | flops 5000000000 | bytes 3000000 | tf_op jit(solution)/shard_map/load/pallas_call | solution.py:183
  2.7 3.9 %collective-permute-start.2 = (f32[8,128]{1,0:T(8,128)S(1)}, f32[8,128]{1,0:T(8,128)S(1)}, u32[]{:S(2)}, u32[]{:S(2)}) collective-permute-start(f32[8,128]{1,0:T(8,128)S(1)} %get-tuple-element.31), channel_id=1, source_target_pairs={{0,1},{2,3},{1,0},{3,2},{4,5},{6,7},{5,4},{7,6},{8,9},{10,11},{9,8... | collective-permute-start | bytes 12296 | tf_op jit(solution)/shard_map/ppermute | solution.py:200
  6.6 1.1 %faces.1 = (bf16[80,512]{1,0:T(8,128)(2,1)S(1)}, bf16[80,512]{1,0:T(8,128)(2,1)S(1)}) custom-call(s32[1,1024]{1,0:T(1,128)S(1)} %get-tuple-element.25.code_ref, bf16[175,1024]{1,0:T(8,128)(2,1)S(1)} %get-tuple-element.33.tet_ref, bf16[320,175]{1,0:T(8,128)(2,1)S(1)} %get-tuple-element.28.pad_ref), custom_call_target="tpu_custom_call" | custom-call | flops 5000000000 | bytes 600000 | tf_op jit(solution)/shard_map/faces/pallas_call | solution.py:183
  7.7 4.0 %collective-permute-start = (bf16[80,512]{1,0:T(8,128)(2,1)S(1)}, bf16[80,512]{1,0:T(8,128)(2,1)S(1)}, u32[]{:S(2)}, u32[]{:S(2)}) collective-permute-start(bf16[80,512]{1,0:T(8,128)(2,1)S(1)} %get-tuple-element.30.up_ref), channel_id=1, source_target_pairs={{0,4},{4,8},{8,12},{12,16},{16,20},{20,24},{24,28},{28,32},{32,36}... | collective-permute-start | bytes 245768 | tf_op jit(solution)/shard_map/ppermute | solution.py:257
  11.8 7.6 %collective-permute-start.1 = (bf16[80,512]{1,0:T(8,128)(2,1)S(1)}, bf16[80,512]{1,0:T(8,128)(2,1)S(1)}, u32[]{:S(2)}, u32[]{:S(2)}) collective-permute-start(bf16[80,512]{1,0:T(8,128)(2,1)S(1)} %get-tuple-element.29.low_ref), channel_id=1, source_target_pairs={{4,0},{8,4},{12,8},{16,12},{20,16},{24,20},{28,24},{32,28},{36,32}... | collective-permute-start | bytes 245768 | tf_op jit(solution)/shard_map/ppermute | solution.py:258
  19.4 0.0 collective-permute-done.2
  19.4 1.9 %collective-permute-start.3 = (f32[8,128]{1,0:T(8,128)S(1)}, f32[8,128]{1,0:T(8,128)S(1)}, u32[]{:S(2)}, u32[]{:S(2)}) collective-permute-start(f32[8,128]{1,0:T(8,128)S(1)} %add.3.pair_ref), channel_id=1, source_target_pairs={{1,2},{0,3},{2,1},{3,0},{5,6},{4,7},{6,5},{7,4},{9,10},{8,11},{10,... | collective-permute-start | bytes 12296 | tf_op jit(solution)/shard_map/ppermute | solution.py:200
  21.4 1.0 %local.1 = (f32[175,1024]{1,0:T(8,128)S(1)}, f32[375,1024]{1,0:T(8,128)S(1)}, f32[75,1024]{1,0:T(8,128)S(1)}, f32[75,1024]{1,0:T(8,128)S(1)}, bf16[175,320]{1,0:T(8,128)(2,1)S(1)}) custom-call(bf16[175,1024]{1,0:T(8,128)(2,1)S(1)} %get-tuple-element.33.tet_ref, bf16[375,1024]{1,0:T(8,128)(2,1)S(1)} %get-tuple-element.34.prism_ref, ...), custom_call_target="tpu_custom_call" | custom-call | flops 5000000000 | bytes 4000000 | tf_op jit(solution)/shard_map/local/pallas_call | solution.py:183
  22.4 0.0 collective-permute-done.from_low_ref
  22.4 0.0 collective-permute-done.1.from_up_ref
  22.4 1.2 %tet_finish.1.tet_ref = bf16[175,1024]{1,0:T(8,128)(2,1)S(1)} custom-call(s32[1,1024]{1,0:T(1,128)S(1)} %get-tuple-element.25.code_ref, f32[1,1024]{1,0:T(1,128)S(1)} %get-tuple-element.26.live_ref, bf16[80,512]{1,0:T(8,128)(2,1)S(1)} %get-tuple-element.29.low_ref, bf16[80,512]{1,0:T(8,128)(2,1)S(1)} %get-tuple-element.30.up_ref, ...), custom_call_target="tpu_custom_call" | custom-call | flops 5000000000 | bytes 3000000 | tf_op jit(solution)/shard_map/tet_finish/pallas_call | solution.py:183
  23.6 1.6 %collective-permute-done.3.other_ref = f32[8,128]{1,0:T(8,128)S(1)} collective-permute-done((f32[8,128]{1,0:T(8,128)S(1)}, f32[8,128]{1,0:T(8,128)S(1)}, u32[]{:S(2)}, u32[]{:S(2)}) %collective-permute-start.3) | collective-permute-done | bytes 4128 | tf_op jit(solution)/shard_map/ppermute | solution.py:200
  25.1 1.2 %prism_finish.1 = (bf16[175,1024]{1,0:T(8,128)(2,1)}, bf16[375,1024]{1,0:T(8,128)(2,1)}) custom-call(bf16[175,1024]{1,0:T(8,128)(2,1)S(1)} %tet_finish.1.tet_ref, f32[8,128]{1,0:T(8,128)S(1)} %add.3.pair_ref, f32[8,128]{1,0:T(8,128)S(1)} %collective-permute-done.3.other_ref, f32[1,4,6]{2,1,0:T(4,128)S(1)} %get-tuple-element.39.law_ref, ...), custom_call_target="tpu_custom_call" | custom-call | flops 5000000000 | bytes 3000000 | tf_op jit(solution)/shard_map/prism_finish/pallas_call | solution.py:183
  (1 shorter events, 0.0 us)
Async XLA Ops:
  2.7 16.7 %collective-permute-start.2 = (f32[8,128]{1,0:T(8,128)S(1)}, f32[8,128]{1,0:T(8,128)S(1)}, u32[]{:S(2)}, u32[]{:S(2)}) collective-permute-start(f32[8,128]{1,0:T(8,128)S(1)} %get-tuple-element.31), channel_id=1, source_target_pairs={{0,1},{2,3},{1,0},{3,2},{4,5},{6,7},{5,4},{7,6},{8,9},{10,11},{9,8... | collective-permute-start | bytes 12296 | tf_op jit(solution)/shard_map/ppermute | solution.py:200
  7.7 14.7 %collective-permute-start = (bf16[80,512]{1,0:T(8,128)(2,1)S(1)}, bf16[80,512]{1,0:T(8,128)(2,1)S(1)}, u32[]{:S(2)}, u32[]{:S(2)}) collective-permute-start(bf16[80,512]{1,0:T(8,128)(2,1)S(1)} %get-tuple-element.30.up_ref), channel_id=1, source_target_pairs={{0,4},{4,8},{8,12},{12,16},{16,20},{20,24},{24,28},{28,32},{32,36}... | collective-permute-start | bytes 245768 | tf_op jit(solution)/shard_map/ppermute | solution.py:257
  11.8 10.6 %collective-permute-start.1 = (bf16[80,512]{1,0:T(8,128)(2,1)S(1)}, bf16[80,512]{1,0:T(8,128)(2,1)S(1)}, u32[]{:S(2)}, u32[]{:S(2)}) collective-permute-start(bf16[80,512]{1,0:T(8,128)(2,1)S(1)} %get-tuple-element.29.low_ref), channel_id=1, source_target_pairs={{4,0},{8,4},{12,8},{16,12},{20,16},{24,20},{28,24},{32,28},{36,32}... | collective-permute-start | bytes 245768 | tf_op jit(solution)/shard_map/ppermute | solution.py:258
  19.4 5.7 %collective-permute-start.3 = (f32[8,128]{1,0:T(8,128)S(1)}, f32[8,128]{1,0:T(8,128)S(1)}, u32[]{:S(2)}, u32[]{:S(2)}) collective-permute-start(f32[8,128]{1,0:T(8,128)S(1)} %add.3.pair_ref), channel_id=1, source_target_pairs={{1,2},{0,3},{2,1},{3,0},{5,6},{4,7},{6,5},{7,4},{9,10},{8,11},{10,... | collective-permute-start | bytes 12296 | tf_op jit(solution)/shard_map/ppermute | solution.py:200

commit v3 on v2

--- a/solution.py
+++ b/solution.py
@@ -59,85 +59,102 @@
     ).astype(BF)
 
 
-def load_kernel(*refs):
-    loads, refs = refs[:14], refs[14:]
-    (part_ref, pad_ref, owned_ref, live_ref), refs = refs[:4], refs[4:]
-    (code_ref, tet_ref, prism_ref, volume_ref, prism_volume_ref, lift_ref, wall_lift_ref, wall_ref, law_ref), refs = refs[:9], refs[9:]
-    burn_ref, owner_ref, extrap_ref, count_ref, area_ref, sems = refs
-    targets = (
-        burn_ref, owner_ref, wall_ref, extrap_ref, prism_ref, code_ref, tet_ref,
-        count_ref, area_ref, law_ref, volume_ref, prism_volume_ref, lift_ref, wall_lift_ref,
-    )
-    copies = [pltpu.make_async_copy(a, b, sems.at[n]) for n, (a, b) in enumerate(zip(loads, targets))]
+def first_side():
+    return 1 - (lax.axis_index("axial") & 1)
+
+
+def side_of(ref, side):
+    width = ref.shape[1] // 2
+    return ref[:, pl.ds(pl.multiple_of(side * width, width), width)]
+
+
+def send_kernel(
+    code_hbm, burn_hbm, owner_hbm, extrap_hbm, wall_hbm, tet_hbm, prism_hbm,
+    part_ref, odd_ref, even_ref, owned_ref, code_ref, wall_ref, tet_ref, prism_ref,
+    burn_ref, owner_ref, extrap_ref, sems,
+):
+    pairs = (
+        (code_hbm, code_ref), (burn_hbm, burn_ref), (owner_hbm, owner_ref), (extrap_hbm, extrap_ref),
+        (wall_hbm, wall_ref), (tet_hbm, tet_ref), (prism_hbm, prism_ref),
+    )
+    copies = [pltpu.make_async_copy(a, b, sems.at[n]) for n, (a, b) in enumerate(pairs)]
     for copy in copies:
         copy.start()
+    spreads = spread(4 * FP, 4 * FW)
     for copy in copies[:4]:
         copy.wait()
-    pad_ref[...] = mm(spread(4 * FP, 4 * FW), extrap_ref[...], NT).astype(BF)
+    pad = mm(spreads, extrap_ref[...], NT).astype(BF)
     walls = burn_ref.shape[1]
     place = hot(rows_of((prism_ref.shape[1], walls)) == burn_ref[...])
     owned = mm(hot(rows_of((8, walls)) == owner_ref[...]), place, NT)
     owned_ref[...] = owned
     for copy in copies[4:]:
         copy.wait()
+    capacity = odd_ref.shape[1]
+    left = faces_of(code_ref[...], tet_ref[...], pad)
+    upper = first_side() == 1
+    odd_ref[...] = jnp.where(upper, left[:, :capacity], left[:, capacity:])
+    even_ref[...] = jnp.where(upper, left[:, capacity:], left[:, :capacity])
     rows = mm(wall_ref[(NV - 1) * TFP : NV * TFP, :], prism_ref[...]).astype(BF).astype(F32)
     sums = jnp.sum(rows * rows, axis=0, keepdims=True)
     part_ref[...] = jnp.broadcast_to(jnp.sum(owned * sums, axis=1, keepdims=True), part_ref.shape)
-    capacity = live_ref.shape[1] // 2
-    slot = cols_of((1, capacity))
-    for side in range(2):
-        area = area_ref[:, side * capacity : (side + 1) * capacity]
-        live_ref[:, side * capacity : (side + 1) * capacity] = jnp.where(slot < count_ref[:, side : side + 1], area, 0.0)
-
-
-def face_kernel(code_ref, tet_ref, pad_ref, low_ref, up_ref):
-    capacity = low_ref.shape[1]
-    state = tet_ref[...]
-    pad = pad_ref[...]
-    low_ref[...] = faces_of(code_ref[:, :capacity], state, pad)
-    up_ref[...] = faces_of(code_ref[:, capacity:], state, pad)
 
 
 def local_kernel(
-    tet_ref, prism_ref, volume_ref, prism_volume_ref, wall_ref, lift_ref, law_ref, owned_ref,
-    tet_part_ref, prism_part_ref, rows_ref, gain_ref, pad_ref,
+    tet_ref, prism_ref, wall_ref, owned_ref, volume_hbm, prism_volume_hbm, lift_hbm, law_hbm, wall_lift_hbm, count_hbm, area_hbm,
+    tet_part_ref, prism_part_ref, rows_ref, gain_ref, pad_ref, live_ref, law_ref, wall_lift_ref,
+    volume_ref, prism_volume_ref, lift_ref, count_ref, area_ref, sems,
 ):
-    state = tet_ref[...]
-    tet_part_ref[...] = state.astype(F32) - STEP * mm(volume_ref[...], square_half(state))
-    pad_ref[...] = mm(lift_ref[...], spread(4 * FP, 4 * FW), NT).astype(BF)
-    state = prism_ref[...]
-    prism_part_ref[...] = state.astype(F32) - STEP * mm(prism_volume_ref[...], square_half(state))
-    rows = mm(wall_ref[...], state).astype(BF).astype(F32)
+    pairs = (
+        (law_hbm, law_ref), (prism_volume_hbm, prism_volume_ref), (volume_hbm, volume_ref), (lift_hbm, lift_ref),
+        (count_hbm, count_ref), (area_hbm, area_ref), (wall_lift_hbm, wall_lift_ref),
+    )
+    copies = [pltpu.make_async_copy(a, b, sems.at[n]) for n, (a, b) in enumerate(pairs)]
+    for copy in copies:
+        copy.start()
+    rows = mm(wall_ref[...], prism_ref[...]).astype(BF).astype(F32)
     elements = rows.shape[1]
+    any_owner = jnp.sum(owned_ref[:SECTORS, :], axis=0, keepdims=True)
+    rows_ref[...] = jnp.where(any_owner > 0.5, rows, 0.0)
     pressure = rows[(NV - 1) * TFP :]
     squares = jnp.concatenate([pressure * pressure] * NV, axis=0)
+    for copy in copies:
+        copy.wait()
     v = rows_of((FW, 128)) // TFP
     weight = jnp.zeros((FW, elements), F32)
-    any_owner = jnp.zeros((1, elements), F32)
     for o in range(SECTORS):
         column = jnp.zeros((FW, 128), F32)
         for k in range(NV):
             gain = law_ref[0, o : o + 1, 1 + k : 2 + k] * law_ref[0, o : o + 1, 0:1]
             column = jnp.where(v == k, gain, column)
         column = jnp.concatenate([column] * (elements // 128), axis=1)
-        owned = owned_ref[o : o + 1, :]
-        any_owner = any_owner + owned
-        weight = jnp.where(owned > 0.5, column, weight)
+        weight = jnp.where(owned_ref[o : o + 1, :] > 0.5, column, weight)
     gain_ref[...] = weight * squares
-    rows_ref[...] = jnp.where(any_owner > 0.5, rows, 0.0)
-
-
-def tet_kernel(code_ref, live_ref, low_ref, up_ref, from_low_ref, from_up_ref, part_ref, pad_ref, out_ref):
-    capacity = low_ref.shape[1]
+    state = prism_ref[...]
+    prism_part_ref[...] = state.astype(F32) - STEP * mm(prism_volume_ref[...], square_half(state))
+    state = tet_ref[...]
+    tet_part_ref[...] = state.astype(F32) - STEP * mm(volume_ref[...], square_half(state))
+    pad_ref[...] = mm(lift_ref[...], spread(4 * FP, 4 * FW), NT).astype(BF)
+    capacity = live_ref.shape[1] // 2
+    slot = cols_of((1, capacity))
+    for side in range(2):
+        area = area_ref[:, side * capacity : (side + 1) * capacity]
+        live_ref[:, side * capacity : (side + 1) * capacity] = jnp.where(slot < count_ref[:, side : side + 1], area, 0.0)
+
+
+def tet_kernel(code_ref, live_ref, odd_ref, even_ref, from_odd_ref, from_even_ref, part_ref, pad_ref, out_ref):
+    first = first_side()
+    capacity = even_ref.shape[1]
     elements = part_ref.shape[1]
     placed = None
-    for side, own, other, normal in ((0, low_ref, from_low_ref, -1.0), (1, up_ref, from_up_ref, 1.0)):
-        code = code_ref[:, side * capacity : (side + 1) * capacity]
-        live = live_ref[:, side * capacity : (side + 1) * capacity]
+    for side, own, other in ((1 - first, odd_ref, from_odd_ref), (first, even_ref, from_even_ref)):
+        code = side_of(code_ref, side)
+        live = side_of(live_ref, side)
+        normal = jnp.where(side == 0, -0.25, 0.25)
         left = own[...].astype(F32)
         right = other[...].astype(F32)
         speed = jnp.maximum(jnp.abs(left), jnp.abs(right))
-        flux = (0.25 * normal) * (right * right - left * left) - 0.5 * speed * (right - left)
+        flux = normal * (right * right - left * left) - 0.5 * speed * (right - left)
         jump = (live * flux).astype(BF)
         face = code & 3
         masked = jnp.concatenate([jnp.where(face == f, jump, jnp.zeros_like(jump)) for f in range(4)], axis=0)
@@ -224,56 +241,50 @@
     owner = burn_owner.reshape(1, -1)
     extrap = face_extrap.T
     wall_lift = wall_lift.T
-    operands = (
-        burn, owner, wall_extrap, extrap, prism_state, code, tet_state,
-        face_count, area, burn_law, tet_volume, prism_volume, face_lift, wall_lift,
-    )
-    kept = (code, tet_state, prism_state, tet_volume, prism_volume, face_lift, wall_lift, wall_extrap, burn_law)
+    tall = prism_state.shape[1]
     side = pltpu.VMEM((FP, capacity), BF)
-    outs = (
-        pltpu.VMEM((8, 128), F32),
-        pltpu.VMEM((4 * FP, tet_state.shape[0]), BF),
-        pltpu.VMEM((8, prism_state.shape[1]), F32),
-        pltpu.VMEM((1, slots), F32),
-    ) + tuple(like(x) for x in kept)
-    part, face_pad, owned, live, code, tet, prism, tet_vol, prism_vol, lift, wall_lift, wall, law = call(
-        load_kernel,
-        "load",
-        outs,
-        (VM,) * len(outs),
-        [HB] * len(operands),
+    hbm = pltpu.with_memory_space_constraint
+    operands = (code, burn, owner, extrap, wall_extrap, tet_state, prism_state)
+    part, odd, even, owned, code, wall, tet, prism = call(
+        send_kernel,
+        "send",
+        (pltpu.VMEM((8, 128), F32), side, side, pltpu.VMEM((8, tall), F32))
+        + tuple(like(x) for x in (code, wall_extrap, tet_state, prism_state)),
+        (VM,) * 8,
+        [HB] * 7,
         5_000_000_000,
         3_000_000,
-        tuple(pltpu.with_memory_space_constraint(x, pltpu.HBM) for x in operands),
-        [like(x) for x in (burn, owner, extrap, face_count, area)]
-        + [pltpu.SemaphoreType.DMA((len(operands),))],
+        tuple(hbm(x, pltpu.HBM) for x in operands),
+        [like(x) for x in (burn, owner, extrap)] + [pltpu.SemaphoreType.DMA((7,))],
     )
     half = swap(part, "azim", ((0, 1), (2, 3)))
-    low, up = call(
-        face_kernel, "faces", (side, side), (VM, VM), [VM] * 3, 5_000_000_000, 600_000, (code, tet, face_pad)
-    )
     count = lax.axis_size("axial")
-    forward = [(i, i + 1) for i in range(count - 1)]
-    from_low = lax.ppermute(up, "axial", forward)
-    from_up = lax.ppermute(low, "axial", [(j, i) for i, j in forward])
+    from_even = swap(even, "axial", [(i, i + 1) for i in range(0, count - 1, 2)])
+    from_odd = swap(odd, "axial", [(i, i + 1) for i in range(1, count - 1, 2)])
     pair = part + half
     other = swap(pair, "azim", ((1, 2), (0, 3)))
     pair, tet, prism = lax.optimization_barrier((pair, tet, prism))
-    tet_part, prism_part, rows, gain, pad = call(
+    operands = (tet_volume, prism_volume, face_lift, burn_law, wall_lift, face_count, area)
+    tet_part, prism_part, rows, gain, pad, live, law, wall_lift = call(
         local_kernel,
         "local",
         (
             pltpu.VMEM(tet.shape, F32),
             pltpu.VMEM(prism.shape, F32),
-            pltpu.VMEM((FW, prism.shape[1]), F32),
-            pltpu.VMEM((FW, prism.shape[1]), F32),
+            pltpu.VMEM((FW, tall), F32),
+            pltpu.VMEM((FW, tall), F32),
             pltpu.VMEM((tet.shape[0], 4 * FP), BF),
+            like(area),
+            like(burn_law),
+            like(wall_lift),
         ),
-        (VM,) * 5,
-        [VM] * 8,
+        (VM,) * 8,
+        [VM] * 4 + [HB] * 7,
         5_000_000_000,
         4_000_000,
-        (tet, prism, tet_vol, prism_vol, wall, lift, law, owned),
+        (tet, prism, wall, owned) + tuple(hbm(x, pltpu.HBM) for x in operands),
+        [like(x) for x in (tet_volume, prism_volume, face_lift, face_count, area)]
+        + [pltpu.SemaphoreType.DMA((7,))],
     )
     tet_new = call(
         tet_kernel,
@@ -283,7 +294,7 @@
         [VM] * 8,
         5_000_000_000,
         3_000_000,
-        (code, live, low, up, from_low, from_up, tet_part, pad),
+        (code, live, odd, even, from_odd, from_even, tet_part, pad),
     )
     tet_new, prism_new = call(
         prism_kernel,

time: 26.6 us -> 25.3 us (0.951)
  waiting for transfers between devices: 1.56 us -> 0.36 us
  starting transfers between devices: 17.6 us -> 16.9 us
  Pallas kernels: 6.54 us -> 7.01 us
    ppermute x2 -> x0, starting transfers between devices: 11.7 us -> none  [the longest x1 7.65 us: on_device(): from_up = lax.ppermute(low, 'axial', [(j, i) for i, j in forward])]
    ppermute x2 -> x4, starting transfers between devices: 5.87 us -> 16.9 us  [swap(): return lax.ppermute(value, axis, list(pairs) + [(j, i) for i, j in pairs])]
    ppermute x2 -> x4, waiting for transfers between devices: 1.55 us -> 0.36 us  [swap(): return lax.ppermute(value, axis, list(pairs) + [(j, i) for i, j in pairs])]
    pallas_call x5 -> x4, Pallas kernels: 6.54 us -> 7.01 us  [call(): pl.pallas_call(kernel, out_shape=outs, in_specs=specs, out_specs=out_spec...]
  transfers between devices with their start and end apart: 4 -> 4, of which waited for: 1 -> 1; matrix products, arithmetic and copies ran while one was open for 0% -> 0% of each run, Pallas kernels for 12% -> 13%
where the time goes in v3:
time: 25.3 us; the launch traced here: 25 us
  starting transfers between devices  16.9 us (67%)
  Pallas kernels  7.01 us (28%)
  between operations  0.72 us (3%)
  waiting for transfers between devices  0.36 us (1%)
    ppermute x4, starting transfers between devices, swap(): return lax.ppermute(value, axis, list(pairs) + [(j, i) for i, j in pairs])  16.9 us
    pallas_call x4, Pallas kernels, call(): pl.pallas_call(kernel, out_shape=outs, in_specs=specs, out_specs=out_spec...  7.01 us
  transfers between devices with their start and end apart: 4, of which 1 were waited for; matrix products, arithmetic and copies ran while one was open for 0% of the time, Pallas kernels for 13%

profile of v3, /device:TPU:1, one launch (start us, length us, event | category | flops | bytes accessed | tf_op | source)
XLA Modules:
  0.0 25.0 jit_solution(5381668721957141709)
XLA Ops:
  0.6 2.5 %send.1 = (f32[8,128]{1,0:T(8,128)S(1)}, bf16[80,512]{1,0:T(8,128)(2,1)S(1)}, bf16[80,512]{1,0:T(8,128)(2,1)S(1)}, f32[8,1024]{1,0:T(8,128)S(1)}, s32[1,1024]{1,...) custom-call(s32[1,1024]{1,0:T(1,128)} %bitcast.8, ...), custom_call_target="tpu_custom_call" | custom-call | flops 5000000000 | bytes 3000000 | tf_op jit(solution)/shard_map/send/pallas_call | solution.py:200
  3.2 4.0 %collective-permute-start = (f32[8,128]{1,0:T(8,128)S(1)}, f32[8,128]{1,0:T(8,128)S(1)}, u32[]{:S(2)}, u32[]{:S(2)}) collective-permute-start(f32[8,128]{1,0:T(8,128)S(1)} %get-tuple-element.22), channel_id=1, source_target_pairs={{0,1},{2,3},{1,0},{3,2},{4,5},{6,7},{5,4},{7,6},{8,9},{10,11},{9,8... | collective-permute-start | bytes 12296 | tf_op jit(solution)/shard_map/ppermute | solution.py:217
  7.1 4.0 %collective-permute-start.1 = (bf16[80,512]{1,0:T(8,128)(2,1)S(1)}, bf16[80,512]{1,0:T(8,128)(2,1)S(1)}, u32[]{:S(2)}, u32[]{:S(2)}) collective-permute-start(bf16[80,512]{1,0:T(8,128)(2,1)S(1)} %get-tuple-element.30.odd_ref), channel_id=1, source_target_pairs={{4,8},{12,16},{20,24},{28,32},{36,40},{44,48},{52,56},{60,64},{68,... | collective-permute-start | bytes 245768 | tf_op jit(solution)/shard_map/ppermute | solution.py:217
  11.2 7.0 %collective-permute-start.2 = (bf16[80,512]{1,0:T(8,128)(2,1)S(1)}, bf16[80,512]{1,0:T(8,128)(2,1)S(1)}, u32[]{:S(2)}, u32[]{:S(2)}) collective-permute-start(bf16[80,512]{1,0:T(8,128)(2,1)S(1)} %get-tuple-element.31.even_ref), channel_id=1, source_target_pairs={{0,4},{8,12},{16,20},{24,28},{32,36},{40,44},{48,52},{56,60},{64,6... | collective-permute-start | bytes 245768 | tf_op jit(solution)/shard_map/ppermute | solution.py:217
  18.2 0.0 collective-permute-done
  18.2 1.9 %collective-permute-start.3 = (f32[8,128]{1,0:T(8,128)S(1)}, f32[8,128]{1,0:T(8,128)S(1)}, u32[]{:S(2)}, u32[]{:S(2)}) collective-permute-start(f32[8,128]{1,0:T(8,128)S(1)} %add.3.pair_ref), channel_id=1, source_target_pairs={{1,2},{0,3},{2,1},{3,0},{5,6},{4,7},{6,5},{7,4},{9,10},{8,11},{10,... | collective-permute-start | bytes 12296 | tf_op jit(solution)/shard_map/ppermute | solution.py:217
  20.1 2.1 %local.1 = (f32[175,1024]{1,0:T(8,128)S(1)}, f32[375,1024]{1,0:T(8,128)S(1)}, f32[75,1024]{1,0:T(8,128)S(1)}, f32[75,1024]{1,0:T(8,128)S(1)}, bf16[175,320]{1,0:...) custom-call(bf16[175,1024]{1,0:T(8,128)(2,1)S(1)} %get-tuple-element.25.tet_ref, ...), custom_call_target="tpu_custom_call" | custom-call | flops 5000000000 | bytes 4000000 | tf_op jit(solution)/shard_map/local/pallas_call | solution.py:200
  22.2 0.0 collective-permute-done.1.from_odd_ref
  22.2 0.0 collective-permute-done.2.from_even_ref
  22.2 1.2 %tet_finish.1.tet_ref = bf16[175,1024]{1,0:T(8,128)(2,1)S(1)} custom-call(s32[1,1024]{1,0:T(1,128)S(1)} %get-tuple-element.21.code_ref, f32[1,1024]{1,0:T(1,128)S(1)} %get-tuple-element.29.live_ref, bf16[80,512]{1,0:T(8,128)(2,1)S(1)} %get-tuple-element.30.odd_ref, bf16[80,512]{1,0:T(8,128)(2,1)S(1)} %get-tuple-element.31.even_ref, ...), custom_call_target="tpu_custom_call" | custom-call | flops 5000000000 | bytes 3000000 | tf_op jit(solution)/shard_map/tet_finish/pallas_call | solution.py:200
  23.4 0.3 %collective-permute-done.3.other_ref = f32[8,128]{1,0:T(8,128)S(1)} collective-permute-done((f32[8,128]{1,0:T(8,128)S(1)}, f32[8,128]{1,0:T(8,128)S(1)}, u32[]{:S(2)}, u32[]{:S(2)}) %collective-permute-start.3) | collective-permute-done | bytes 4128 | tf_op jit(solution)/shard_map/ppermute | solution.py:217
  23.8 1.2 %prism_finish.1 = (bf16[175,1024]{1,0:T(8,128)(2,1)}, bf16[375,1024]{1,0:T(8,128)(2,1)}) custom-call(bf16[175,1024]{1,0:T(8,128)(2,1)S(1)} %tet_finish.1.tet_ref, f32[8,128]{1,0:T(8,128)S(1)} %add.3.pair_ref, f32[8,128]{1,0:T(8,128)S(1)} %collective-permute-done.3.other_ref, f32[1,4,6]{2,1,0:T(4,128)S(1)} %get-tuple-element.35.law_ref, ...), custom_call_target="tpu_custom_call" | custom-call | flops 5000000000 | bytes 3000000 | tf_op jit(solution)/shard_map/prism_finish/pallas_call | solution.py:200
  (1 shorter events, 0.0 us)
Async XLA Ops:
  3.2 15.0 %collective-permute-start = (f32[8,128]{1,0:T(8,128)S(1)}, f32[8,128]{1,0:T(8,128)S(1)}, u32[]{:S(2)}, u32[]{:S(2)}) collective-permute-start(f32[8,128]{1,0:T(8,128)S(1)} %get-tuple-element.22), channel_id=1, source_target_pairs={{0,1},{2,3},{1,0},{3,2},{4,5},{6,7},{5,4},{7,6},{8,9},{10,11},{9,8... | collective-permute-start | bytes 12296 | tf_op jit(solution)/shard_map/ppermute | solution.py:217
  7.1 15.1 %collective-permute-start.1 = (bf16[80,512]{1,0:T(8,128)(2,1)S(1)}, bf16[80,512]{1,0:T(8,128)(2,1)S(1)}, u32[]{:S(2)}, u32[]{:S(2)}) collective-permute-start(bf16[80,512]{1,0:T(8,128)(2,1)S(1)} %get-tuple-element.30.odd_ref), channel_id=1, source_target_pairs={{4,8},{12,16},{20,24},{28,32},{36,40},{44,48},{52,56},{60,64},{68,... | collective-permute-start | bytes 245768 | tf_op jit(solution)/shard_map/ppermute | solution.py:217
  11.2 11.1 %collective-permute-start.2 = (bf16[80,512]{1,0:T(8,128)(2,1)S(1)}, bf16[80,512]{1,0:T(8,128)(2,1)S(1)}, u32[]{:S(2)}, u32[]{:S(2)}) collective-permute-start(bf16[80,512]{1,0:T(8,128)(2,1)S(1)} %get-tuple-element.31.even_ref), channel_id=1, source_target_pairs={{0,4},{8,12},{16,20},{24,28},{32,36},{40,44},{48,52},{56,60},{64,6... | collective-permute-start | bytes 245768 | tf_op jit(solution)/shard_map/ppermute | solution.py:217
  18.2 5.6 %collective-permute-start.3 = (f32[8,128]{1,0:T(8,128)S(1)}, f32[8,128]{1,0:T(8,128)S(1)}, u32[]{:S(2)}, u32[]{:S(2)}) collective-permute-start(f32[8,128]{1,0:T(8,128)S(1)} %add.3.pair_ref), channel_id=1, source_target_pairs={{1,2},{0,3},{2,1},{3,0},{5,6},{4,7},{6,5},{7,4},{9,10},{8,11},{10,... | collective-permute-start | bytes 12296 | tf_op jit(solution)/shard_map/ppermute | solution.py:217

commit v4 on v3

--- a/solution.py
+++ b/solution.py
@@ -68,14 +68,14 @@
     return ref[:, pl.ds(pl.multiple_of(side * width, width), width)]
 
 
-def send_kernel(
-    code_hbm, burn_hbm, owner_hbm, extrap_hbm, wall_hbm, tet_hbm, prism_hbm,
-    part_ref, odd_ref, even_ref, owned_ref, code_ref, wall_ref, tet_ref, prism_ref,
+def wall_kernel(
+    burn_hbm, owner_hbm, wall_hbm, prism_hbm, extrap_hbm, code_hbm, tet_hbm,
+    part_ref, pad_ref, owned_ref, code_ref, wall_ref, tet_ref, prism_ref,
     burn_ref, owner_ref, extrap_ref, sems,
 ):
     pairs = (
-        (code_hbm, code_ref), (burn_hbm, burn_ref), (owner_hbm, owner_ref), (extrap_hbm, extrap_ref),
-        (wall_hbm, wall_ref), (tet_hbm, tet_ref), (prism_hbm, prism_ref),
+        (burn_hbm, burn_ref), (owner_hbm, owner_ref), (wall_hbm, wall_ref), (extrap_hbm, extrap_ref),
+        (prism_hbm, prism_ref), (code_hbm, code_ref), (tet_hbm, tet_ref),
     )
     copies = [pltpu.make_async_copy(a, b, sems.at[n]) for n, (a, b) in enumerate(pairs)]
     for copy in copies:
@@ -83,43 +83,36 @@
     spreads = spread(4 * FP, 4 * FW)
     for copy in copies[:4]:
         copy.wait()
-    pad = mm(spreads, extrap_ref[...], NT).astype(BF)
+    pad_ref[...] = mm(spreads, extrap_ref[...], NT).astype(BF)
     walls = burn_ref.shape[1]
     place = hot(rows_of((prism_ref.shape[1], walls)) == burn_ref[...])
     owned = mm(hot(rows_of((8, walls)) == owner_ref[...]), place, NT)
     owned_ref[...] = owned
     for copy in copies[4:]:
         copy.wait()
+    rows = mm(wall_ref[(NV - 1) * TFP : NV * TFP, :], prism_ref[...]).astype(BF).astype(F32)
+    sums = jnp.sum(rows * rows, axis=0, keepdims=True)
+    part_ref[...] = jnp.broadcast_to(jnp.sum(owned * sums, axis=1, keepdims=True), part_ref.shape)
+
+
+def face_kernel(code_ref, tet_ref, pad_ref, odd_ref, even_ref):
     capacity = odd_ref.shape[1]
-    left = faces_of(code_ref[...], tet_ref[...], pad)
+    left = faces_of(code_ref[...], tet_ref[...], pad_ref[...])
     upper = first_side() == 1
     odd_ref[...] = jnp.where(upper, left[:, :capacity], left[:, capacity:])
     even_ref[...] = jnp.where(upper, left[:, capacity:], left[:, :capacity])
-    rows = mm(wall_ref[(NV - 1) * TFP : NV * TFP, :], prism_ref[...]).astype(BF).astype(F32)
-    sums = jnp.sum(rows * rows, axis=0, keepdims=True)
-    part_ref[...] = jnp.broadcast_to(jnp.sum(owned * sums, axis=1, keepdims=True), part_ref.shape)
 
 
 def local_kernel(
-    tet_ref, prism_ref, wall_ref, owned_ref, volume_hbm, prism_volume_hbm, lift_hbm, law_hbm, wall_lift_hbm, count_hbm, area_hbm,
-    tet_part_ref, prism_part_ref, rows_ref, gain_ref, pad_ref, live_ref, law_ref, wall_lift_ref,
-    volume_ref, prism_volume_ref, lift_ref, count_ref, area_ref, sems,
+    tet_ref, prism_ref, wall_ref, owned_ref, volume_ref, prism_volume_ref, lift_ref, law_ref, count_ref, area_ref,
+    tet_part_ref, prism_part_ref, rows_ref, gain_ref, pad_ref, live_ref,
 ):
-    pairs = (
-        (law_hbm, law_ref), (prism_volume_hbm, prism_volume_ref), (volume_hbm, volume_ref), (lift_hbm, lift_ref),
-        (count_hbm, count_ref), (area_hbm, area_ref), (wall_lift_hbm, wall_lift_ref),
-    )
-    copies = [pltpu.make_async_copy(a, b, sems.at[n]) for n, (a, b) in enumerate(pairs)]
-    for copy in copies:
-        copy.start()
     rows = mm(wall_ref[...], prism_ref[...]).astype(BF).astype(F32)
     elements = rows.shape[1]
     any_owner = jnp.sum(owned_ref[:SECTORS, :], axis=0, keepdims=True)
     rows_ref[...] = jnp.where(any_owner > 0.5, rows, 0.0)
     pressure = rows[(NV - 1) * TFP :]
     squares = jnp.concatenate([pressure * pressure] * NV, axis=0)
-    for copy in copies:
-        copy.wait()
     v = rows_of((FW, 128)) // TFP
     weight = jnp.zeros((FW, elements), F32)
     for o in range(SECTORS):
@@ -244,28 +237,37 @@
     tall = prism_state.shape[1]
     side = pltpu.VMEM((FP, capacity), BF)
     hbm = pltpu.with_memory_space_constraint
-    operands = (code, burn, owner, extrap, wall_extrap, tet_state, prism_state)
-    part, odd, even, owned, code, wall, tet, prism = call(
-        send_kernel,
-        "send",
-        (pltpu.VMEM((8, 128), F32), side, side, pltpu.VMEM((8, tall), F32))
+    operands = (burn, owner, wall_extrap, prism_state, extrap, code, tet_state)
+    part, face_pad, owned, code, wall, tet, prism = call(
+        wall_kernel,
+        "walls",
+        (
+            pltpu.VMEM((8, 128), F32),
+            pltpu.VMEM((4 * FP, tet_state.shape[0]), BF),
+            pltpu.VMEM((8, tall), F32),
+        )
         + tuple(like(x) for x in (code, wall_extrap, tet_state, prism_state)),
-        (VM,) * 8,
+        (VM,) * 7,
         [HB] * 7,
         5_000_000_000,
         3_000_000,
         tuple(hbm(x, pltpu.HBM) for x in operands),
         [like(x) for x in (burn, owner, extrap)] + [pltpu.SemaphoreType.DMA((7,))],
     )
-    half = swap(part, "azim", ((0, 1), (2, 3)))
+    odd, even = call(
+        face_kernel, "faces", (side, side), (VM, VM), [VM] * 3, 5_000_000_000, 600_000, (code, tet, face_pad)
+    )
+    part, tet_volume, prism_volume, face_lift, wall_lift, law, face_count, area = lax.optimization_barrier(
+        (part, tet_volume, prism_volume, face_lift, wall_lift, burn_law, face_count, area)
+    )
+    half = swap(part, "azim", ((0, 3), (1, 2)))
     count = lax.axis_size("axial")
     from_even = swap(even, "axial", [(i, i + 1) for i in range(0, count - 1, 2)])
     from_odd = swap(odd, "axial", [(i, i + 1) for i in range(1, count - 1, 2)])
     pair = part + half
-    other = swap(pair, "azim", ((1, 2), (0, 3)))
+    other = swap(pair, "azim", ((0, 1), (2, 3)))
     pair, tet, prism = lax.optimization_barrier((pair, tet, prism))
-    operands = (tet_volume, prism_volume, face_lift, burn_law, wall_lift, face_count, area)
-    tet_part, prism_part, rows, gain, pad, live, law, wall_lift = call(
+    tet_part, prism_part, rows, gain, pad, live = call(
         local_kernel,
         "local",
         (
@@ -275,16 +277,12 @@
             pltpu.VMEM((FW, tall), F32),
             pltpu.VMEM((tet.shape[0], 4 * FP), BF),
             like(area),
-            like(burn_law),
-            like(wall_lift),
         ),
-        (VM,) * 8,
-        [VM] * 4 + [HB] * 7,
+        (VM,) * 6,
+        [VM] * 10,
         5_000_000_000,
         4_000_000,
-        (tet, prism, wall, owned) + tuple(hbm(x, pltpu.HBM) for x in operands),
-        [like(x) for x in (tet_volume, prism_volume, face_lift, face_count, area)]
-        + [pltpu.SemaphoreType.DMA((7,))],
+        (tet, prism, wall, owned, tet_volume, prism_volume, face_lift, law, face_count, area),
     )
     tet_new = call(
         tet_kernel,

time: 25.3 us -> 24.8 us (0.980)
  the two profiles are of different devices: /device:TPU:1 before, /device:TPU:5 now
where the time goes in v4:
time: 24.8 us; the launch traced here: 24.6 us
  starting transfers between devices  17.5 us (71%)
  Pallas kernels  6.22 us (25%)
  between operations  0.84 us (3%)
    ppermute x4, starting transfers between devices, swap(): return lax.ppermute(value, axis, list(pairs) + [(j, i) for i, j in pairs])  17.5 us
    pallas_call x5, Pallas kernels, call(): pl.pallas_call(kernel, out_shape=outs, in_specs=specs, out_specs=out_spec...  6.22 us
  transfers between devices with their start and end apart: 4, of which 0 were waited for; matrix products, arithmetic and copies ran while one was open for 0% of the time, Pallas kernels for 12%

profile of v4, /device:TPU:5, one launch (start us, length us, event | category | flops | bytes accessed | tf_op | source)
XLA Modules:
  0.0 24.6 jit_solution(1441817355165676816)
XLA Ops:
  0.6 1.9 %walls.1 = (f32[8,128]{1,0:T(8,128)S(1)}, bf16[320,175]{1,0:T(8,128)(2,1)S(1)}, f32[8,1024]{1,0:T(8,128)S(1)}, s32[1,1024]{1,0:T(1,128)S(1)}, bf16[75,375]{1,0:T...) custom-call(s32[1,512]{1,0:T(1,128)} %bitcast.10, s32[1,512]{1,0:T(1,128)} %bitcast.11, ...), custom_call_target="tpu_custom_call" | custom-call | flops 5000000000 | bytes 3000000 | tf_op jit(solution)/shard_map/walls/pallas_call | solution.py:193
  2.6 2.2 %collective-permute-start = (f32[8,128]{1,0:T(8,128)S(1)}, f32[8,128]{1,0:T(8,128)S(1)}, u32[]{:S(2)}, u32[]{:S(2)}) collective-permute-start(f32[8,128]{1,0:T(8,128)S(1)} %get-tuple-element.30), channel_id=1, source_target_pairs={{0,3},{1,2},{3,0},{2,1},{4,7},{5,6},{7,4},{6,5},{8,11},{9,10},{11,... | collective-permute-start | bytes 12296 | tf_op jit(solution)/shard_map/ppermute | solution.py:210
  4.8 0.0 copy-start
  4.8 0.0 copy-start.1
  4.8 0.0 copy-start.2
  4.8 0.0 copy-start.4
  4.8 0.0 copy-start.5
  4.8 0.0 copy-start.6
  4.8 0.8 %faces.1 = (bf16[80,512]{1,0:T(8,128)(2,1)S(1)}, bf16[80,512]{1,0:T(8,128)(2,1)S(1)}) custom-call(s32[1,1024]{1,0:T(1,128)S(1)} %get-tuple-element.28.code_ref, bf16[175,1024]{1,0:T(8,128)(2,1)S(1)} %get-tuple-element.33.tet_ref, bf16[320,175]{1,0:T(8,128)(2,1)S(1)} %get-tuple-element.44.pad_ref), custom_call_target="tpu_custom_call" | custom-call | flops 5000000000 | bytes 600000 | tf_op jit(solution)/shard_map/faces/pallas_call | solution.py:193
  5.7 4.0 %collective-permute-start.1 = (bf16[80,512]{1,0:T(8,128)(2,1)S(1)}, bf16[80,512]{1,0:T(8,128)(2,1)S(1)}, u32[]{:S(2)}, u32[]{:S(2)}) collective-permute-start(bf16[80,512]{1,0:T(8,128)(2,1)S(1)} %get-tuple-element.45.odd_ref), channel_id=1, source_target_pairs={{4,8},{12,16},{20,24},{28,32},{36,40},{44,48},{52,56},{60,64},{68,... | collective-permute-start | bytes 245768 | tf_op jit(solution)/shard_map/ppermute | solution.py:210
  9.7 1.9 %collective-permute-start.2 = (bf16[80,512]{1,0:T(8,128)(2,1)S(1)}, bf16[80,512]{1,0:T(8,128)(2,1)S(1)}, u32[]{:S(2)}, u32[]{:S(2)}) collective-permute-start(bf16[80,512]{1,0:T(8,128)(2,1)S(1)} %get-tuple-element.46.even_ref), channel_id=1, source_target_pairs={{0,4},{8,12},{16,20},{24,28},{32,36},{40,44},{48,52},{56,60},{64,6... | collective-permute-start | bytes 245768 | tf_op jit(solution)/shard_map/ppermute | solution.py:210
  11.6 0.0 collective-permute-done
  11.7 9.3 %collective-permute-start.3 = (f32[8,128]{1,0:T(8,128)S(1)}, f32[8,128]{1,0:T(8,128)S(1)}, u32[]{:S(2)}, u32[]{:S(2)}) collective-permute-start(f32[8,128]{1,0:T(8,128)S(1)} %add.3.pair_ref), channel_id=1, source_target_pairs={{0,1},{2,3},{1,0},{3,2},{4,5},{6,7},{5,4},{7,6},{8,9},{10,11},{9,8... | collective-permute-start | bytes 12296 | tf_op jit(solution)/shard_map/ppermute | solution.py:210
  21.0 0.0 copy-done
  21.0 0.0 copy-done.1
  21.0 0.0 copy-done.2
  21.0 0.0 copy-done.4
  21.1 0.0 copy-done.5
  21.1 0.0 copy-done.6
  21.1 1.0 %local.1 = (f32[175,1024]{1,0:T(8,128)S(1)}, f32[375,1024]{1,0:T(8,128)S(1)}, f32[75,1024]{1,0:T(8,128)S(1)}, f32[75,1024]{1,0:T(8,128)S(1)}, bf16[175,320]{1,0:T(8,128)(2,1)S(1)}, /*index=5*/f32[1,1024]{1,0:T(1,128)S(1)}) custom-call(bf16[175,1024]{1,0:T(8,128)(2,1)S(1)} %get-tuple-element.33.tet_ref, bf16[375,1024]{1,0:T(8,128)(2,1)S(1)} %get-tuple-element.34.prism_ref, ...), custom_call_target="tpu_custom_call" | custom-call | flops 5000000000 | bytes 4000000 | tf_op jit(solution)/shard_map/local/pallas_call | solution.py:193
  22.1 0.0 collective-permute-done.1.from_odd_ref
  22.1 0.0 collective-permute-done.2.from_even_ref
  22.1 0.0 copy-start.3
  22.1 1.2 %tet_finish.1.tet_ref = bf16[175,1024]{1,0:T(8,128)(2,1)S(1)} custom-call(s32[1,1024]{1,0:T(1,128)S(1)} %get-tuple-element.28.code_ref, f32[1,1024]{1,0:T(1,128)S(1)} %get-tuple-element.43.live_ref, bf16[80,512]{1,0:T(8,128)(2,1)S(1)} %get-tuple-element.45.odd_ref, bf16[80,512]{1,0:T(8,128)(2,1)S(1)} %get-tuple-element.46.even_ref, ...), custom_call_target="tpu_custom_call" | custom-call | flops 5000000000 | bytes 3000000 | tf_op jit(solution)/shard_map/tet_finish/pallas_call | solution.py:193
  23.3 0.0 collective-permute-done.3.other_ref
  23.3 0.0 copy-done.3
  23.3 1.2 %prism_finish.1 = (bf16[175,1024]{1,0:T(8,128)(2,1)}, bf16[375,1024]{1,0:T(8,128)(2,1)}) custom-call(bf16[175,1024]{1,0:T(8,128)(2,1)S(1)} %tet_finish.1.tet_ref, f32[8,128]{1,0:T(8,128)S(1)} %add.3.pair_ref, f32[8,128]{1,0:T(8,128)S(1)} %collective-permute-done.3.other_ref, f32[1,4,6]{2,1,0:T(4,128)S(1)} %copy-done.5, ...), custom_call_target="tpu_custom_call" | custom-call | flops 5000000000 | bytes 3000000 | tf_op jit(solution)/shard_map/prism_finish/pallas_call | solution.py:193
  (1 shorter events, 0.0 us)
Async XLA Ops:
  2.6 9.1 %collective-permute-start = (f32[8,128]{1,0:T(8,128)S(1)}, f32[8,128]{1,0:T(8,128)S(1)}, u32[]{:S(2)}, u32[]{:S(2)}) collective-permute-start(f32[8,128]{1,0:T(8,128)S(1)} %get-tuple-element.30), channel_id=1, source_target_pairs={{0,3},{1,2},{3,0},{2,1},{4,7},{5,6},{7,4},{6,5},{8,11},{9,10},{11,... | collective-permute-start | bytes 12296 | tf_op jit(solution)/shard_map/ppermute | solution.py:210
  4.8 16.3 %copy-start = (bf16[375,375]{1,0:T(8,128)(2,1)S(1)}, bf16[375,375]{1,0:T(8,128)(2,1)}, u32[]{:S(2)}) copy-start(bf16[375,375]{1,0:T(8,128)(2,1)} %prism_volume_ref) | copy-start | bytes 843754
  4.8 16.3 %copy-start.1 = (bf16[175,300]{1,0:T(8,128)(2,1)S(1)}, bf16[175,300]{1,0:T(8,128)(2,1)}, u32[]{:S(2)}) copy-start(bf16[175,300]{1,0:T(8,128)(2,1)} %lift_ref) | copy-start | bytes 315004
  4.8 16.3 %copy-start.2 = (bf16[175,175]{1,0:T(8,128)(2,1)S(1)}, bf16[175,175]{1,0:T(8,128)(2,1)}, u32[]{:S(2)}) copy-start(bf16[175,175]{1,0:T(8,128)(2,1)} %volume_ref) | copy-start | bytes 183754
  4.8 16.3 %copy-start.4 = (f32[1024]{0:T(1024)S(1)}, f32[1024]{0:T(1024)}, u32[]{:S(2)}) copy-start(f32[1024]{0:T(1024)} %param.24) | copy-start | bytes 12292
  4.8 16.3 %copy-start.5 = (f32[1,4,6]{2,1,0:T(4,128)S(1)}, f32[1,4,6]{2,1,0:T(4,128)}, u32[]{:S(2)}) copy-start(f32[1,4,6]{2,1,0:T(4,128)} %law_ref.1) | copy-start | bytes 292
  4.8 16.2 %copy-start.6 = (s32[1,2]{1,0:T(1,128)S(1)}, s32[1,2]{1,0:T(1,128)}, u32[]{:S(2)}) copy-start(s32[1,2]{1,0:T(1,128)} %count_ref) | copy-start | bytes 28
  5.7 16.5 %collective-permute-start.1 = (bf16[80,512]{1,0:T(8,128)(2,1)S(1)}, bf16[80,512]{1,0:T(8,128)(2,1)S(1)}, u32[]{:S(2)}, u32[]{:S(2)}) collective-permute-start(bf16[80,512]{1,0:T(8,128)(2,1)S(1)} %get-tuple-element.45.odd_ref), channel_id=1, source_target_pairs={{4,8},{12,16},{20,24},{28,32},{36,40},{44,48},{52,56},{60,64},{68,... | collective-permute-start | bytes 245768 | tf_op jit(solution)/shard_map/ppermute | solution.py:210
  9.7 12.4 %collective-permute-start.2 = (bf16[80,512]{1,0:T(8,128)(2,1)S(1)}, bf16[80,512]{1,0:T(8,128)(2,1)S(1)}, u32[]{:S(2)}, u32[]{:S(2)}) collective-permute-start(bf16[80,512]{1,0:T(8,128)(2,1)S(1)} %get-tuple-element.46.even_ref), channel_id=1, source_target_pairs={{0,4},{8,12},{16,20},{24,28},{32,36},{40,44},{48,52},{56,60},{64,6... | collective-permute-start | bytes 245768 | tf_op jit(solution)/shard_map/ppermute | solution.py:210
  11.7 11.7 %collective-permute-start.3 = (f32[8,128]{1,0:T(8,128)S(1)}, f32[8,128]{1,0:T(8,128)S(1)}, u32[]{:S(2)}, u32[]{:S(2)}) collective-permute-start(f32[8,128]{1,0:T(8,128)S(1)} %add.3.pair_ref), channel_id=1, source_target_pairs={{0,1},{2,3},{1,0},{3,2},{4,5},{6,7},{5,4},{7,6},{8,9},{10,11},{9,8... | collective-permute-start | bytes 12296 | tf_op jit(solution)/shard_map/ppermute | solution.py:210
  22.1 1.2 %copy-start.3 = (bf16[375,75]{0,1:T(8,128)(2,1)S(1)}, bf16[375,75]{0,1:T(8,128)(2,1)}, u32[]{:S(2)}) copy-start(bf16[375,75]{0,1:T(8,128)(2,1)} %param.21) | copy-start | bytes 168754

commit v5 on v4

--- a/solution.py
+++ b/solution.py
@@ -69,35 +69,36 @@
 
 
 def wall_kernel(
-    burn_hbm, owner_hbm, wall_hbm, prism_hbm, extrap_hbm, code_hbm, tet_hbm,
-    part_ref, pad_ref, owned_ref, code_ref, wall_ref, tet_ref, prism_ref,
-    burn_ref, owner_ref, extrap_ref, sems,
+    burn_hbm, owner_hbm, prism_hbm, wall_hbm, tet_hbm, code_hbm, extrap_hbm,
+    part_ref, owned_ref, prism_ref, wall_ref, tet_ref, code_ref, extrap_ref,
+    burn_ref, owner_ref, sems,
 ):
     pairs = (
-        (burn_hbm, burn_ref), (owner_hbm, owner_ref), (wall_hbm, wall_ref), (extrap_hbm, extrap_ref),
-        (prism_hbm, prism_ref), (code_hbm, code_ref), (tet_hbm, tet_ref),
+        (burn_hbm, burn_ref), (owner_hbm, owner_ref), (prism_hbm, prism_ref), (wall_hbm, wall_ref),
+        (tet_hbm, tet_ref), (code_hbm, code_ref), (extrap_hbm, extrap_ref),
     )
     copies = [pltpu.make_async_copy(a, b, sems.at[n]) for n, (a, b) in enumerate(pairs)]
     for copy in copies:
         copy.start()
-    spreads = spread(4 * FP, 4 * FW)
-    for copy in copies[:4]:
+    for copy in copies[:2]:
         copy.wait()
-    pad_ref[...] = mm(spreads, extrap_ref[...], NT).astype(BF)
     walls = burn_ref.shape[1]
     place = hot(rows_of((prism_ref.shape[1], walls)) == burn_ref[...])
     owned = mm(hot(rows_of((8, walls)) == owner_ref[...]), place, NT)
     owned_ref[...] = owned
-    for copy in copies[4:]:
+    for copy in copies[2:4]:
         copy.wait()
     rows = mm(wall_ref[(NV - 1) * TFP : NV * TFP, :], prism_ref[...]).astype(BF).astype(F32)
     sums = jnp.sum(rows * rows, axis=0, keepdims=True)
     part_ref[...] = jnp.broadcast_to(jnp.sum(owned * sums, axis=1, keepdims=True), part_ref.shape)
-
-
-def face_kernel(code_ref, tet_ref, pad_ref, odd_ref, even_ref):
+    for copy in copies[4:]:
+        copy.wait()
+
+
+def face_kernel(code_ref, tet_ref, extrap_ref, odd_ref, even_ref):
     capacity = odd_ref.shape[1]
-    left = faces_of(code_ref[...], tet_ref[...], pad_ref[...])
+    pad = mm(spread(4 * FP, 4 * FW), extrap_ref[...], NT).astype(BF)
+    left = faces_of(code_ref[...], tet_ref[...], pad)
     upper = first_side() == 1
     odd_ref[...] = jnp.where(upper, left[:, :capacity], left[:, capacity:])
     even_ref[...] = jnp.where(upper, left[:, capacity:], left[:, :capacity])
@@ -237,25 +238,20 @@
     tall = prism_state.shape[1]
     side = pltpu.VMEM((FP, capacity), BF)
     hbm = pltpu.with_memory_space_constraint
-    operands = (burn, owner, wall_extrap, prism_state, extrap, code, tet_state)
-    part, face_pad, owned, code, wall, tet, prism = call(
+    operands = (burn, owner, prism_state, wall_extrap, tet_state, code, extrap)
+    part, owned, prism, wall, tet, code, extrap = call(
         wall_kernel,
         "walls",
-        (
-            pltpu.VMEM((8, 128), F32),
-            pltpu.VMEM((4 * FP, tet_state.shape[0]), BF),
-            pltpu.VMEM((8, tall), F32),
-        )
-        + tuple(like(x) for x in (code, wall_extrap, tet_state, prism_state)),
+        (pltpu.VMEM((8, 128), F32), pltpu.VMEM((8, tall), F32)) + tuple(like(x) for x in operands[2:]),
         (VM,) * 7,
         [HB] * 7,
         5_000_000_000,
         3_000_000,
         tuple(hbm(x, pltpu.HBM) for x in operands),
-        [like(x) for x in (burn, owner, extrap)] + [pltpu.SemaphoreType.DMA((7,))],
+        [like(x) for x in operands[:2]] + [pltpu.SemaphoreType.DMA((7,))],
     )
     odd, even = call(
-        face_kernel, "faces", (side, side), (VM, VM), [VM] * 3, 5_000_000_000, 600_000, (code, tet, face_pad)
+        face_kernel, "faces", (side, side), (VM, VM), [VM] * 3, 5_000_000_000, 600_000, (code, tet, extrap)
     )
     part, tet_volume, prism_volume, face_lift, wall_lift, law, face_count, area = lax.optimization_barrier(
         (part, tet_volume, prism_volume, face_lift, wall_lift, burn_law, face_count, area)

time: 24.8 us -> 24.5 us (0.988)
  Pallas kernels: 6.22 us -> 5.94 us
    pallas_call x5, Pallas kernels: 6.22 us -> 5.94 us  [call(): pl.pallas_call(kernel, out_shape=outs, in_specs=specs, out_specs=out_spec...]
  transfers between devices with their start and end apart: 4 -> 4, of which waited for: 0 -> 0; matrix products, arithmetic and copies ran while one was open for 0% -> 0% of each run, Pallas kernels for 12% -> 13%
where the time goes in v5:
time: 24.5 us; the launch traced here: 24.3 us
  starting transfers between devices  17.5 us (71%)
  Pallas kernels  5.94 us (24%)
  between operations  0.84 us (3%)
    ppermute x4, starting transfers between devices, swap(): return lax.ppermute(value, axis, list(pairs) + [(j, i) for i, j in pairs])  17.5 us
    pallas_call x5, Pallas kernels, call(): pl.pallas_call(kernel, out_shape=outs, in_specs=specs, out_specs=out_spec...  5.94 us
  transfers between devices with their start and end apart: 4, of which 0 were waited for; matrix products, arithmetic and copies ran while one was open for 0% of the time, Pallas kernels for 13%

profile of v5, /device:TPU:5, one launch (start us, length us, event | category | flops | bytes accessed | tf_op | source)
XLA Modules:
  0.0 24.3 jit_solution(13172301545909885767)
XLA Ops:
  0.6 1.5 %walls.1 = (f32[8,128]{1,0:T(8,128)S(1)}, f32[8,1024]{1,0:T(8,128)S(1)}, bf16[375,1024]{1,0:T(8,128)(2,1)S(1)}, bf16[75,375]{1,0:T(8,128)(2,1)S(1)}, bf16[175,10...) custom-call(s32[1,512]{1,0:T(1,128)} %bitcast.10, s32[1,512]{1,0:T(1,128)} %bitcast.11, ...), custom_call_target="tpu_custom_call" | custom-call | flops 5000000000 | bytes 3000000 | tf_op jit(solution)/shard_map/walls/pallas_call | solution.py:194
  2.2 2.2 %collective-permute-start = (f32[8,128]{1,0:T(8,128)S(1)}, f32[8,128]{1,0:T(8,128)S(1)}, u32[]{:S(2)}, u32[]{:S(2)}) collective-permute-start(f32[8,128]{1,0:T(8,128)S(1)} %get-tuple-element.30), channel_id=1, source_target_pairs={{0,3},{1,2},{3,0},{2,1},{4,7},{5,6},{7,4},{6,5},{8,11},{9,10},{11,... | collective-permute-start | bytes 12296 | tf_op jit(solution)/shard_map/ppermute | solution.py:211
  4.3 0.0 copy-start
  4.4 0.0 copy-start.1
  4.4 0.0 copy-start.2
  4.4 0.0 copy-start.4
  4.4 0.0 copy-start.5
  4.4 0.0 copy-start.6
  4.4 0.9 %faces.1 = (bf16[80,512]{1,0:T(8,128)(2,1)S(1)}, bf16[80,512]{1,0:T(8,128)(2,1)S(1)}) custom-call(s32[1,1024]{1,0:T(1,128)S(1)} %get-tuple-element.28.code_ref, bf16[175,1024]{1,0:T(8,128)(2,1)S(1)} %get-tuple-element.33.tet_ref, bf16[175,300]{1,0:T(8,128)(2,1)S(1)} %get-tuple-element.44.extrap_ref), custom_call_target="tpu_custom_call" | custom-call | flops 5000000000 | bytes 600000 | tf_op jit(solution)/shard_map/faces/pallas_call | solution.py:194
  5.4 4.0 %collective-permute-start.1 = (bf16[80,512]{1,0:T(8,128)(2,1)S(1)}, bf16[80,512]{1,0:T(8,128)(2,1)S(1)}, u32[]{:S(2)}, u32[]{:S(2)}) collective-permute-start(bf16[80,512]{1,0:T(8,128)(2,1)S(1)} %get-tuple-element.45.odd_ref), channel_id=1, source_target_pairs={{4,8},{12,16},{20,24},{28,32},{36,40},{44,48},{52,56},{60,64},{68,... | collective-permute-start | bytes 245768 | tf_op jit(solution)/shard_map/ppermute | solution.py:211
  9.4 1.9 %collective-permute-start.2 = (bf16[80,512]{1,0:T(8,128)(2,1)S(1)}, bf16[80,512]{1,0:T(8,128)(2,1)S(1)}, u32[]{:S(2)}, u32[]{:S(2)}) collective-permute-start(bf16[80,512]{1,0:T(8,128)(2,1)S(1)} %get-tuple-element.46.even_ref), channel_id=1, source_target_pairs={{0,4},{8,12},{16,20},{24,28},{32,36},{40,44},{48,52},{56,60},{64,6... | collective-permute-start | bytes 245768 | tf_op jit(solution)/shard_map/ppermute | solution.py:211
  11.3 0.0 collective-permute-done
  11.4 9.3 %collective-permute-start.3 = (f32[8,128]{1,0:T(8,128)S(1)}, f32[8,128]{1,0:T(8,128)S(1)}, u32[]{:S(2)}, u32[]{:S(2)}) collective-permute-start(f32[8,128]{1,0:T(8,128)S(1)} %add.3.pair_ref), channel_id=1, source_target_pairs={{0,1},{2,3},{1,0},{3,2},{4,5},{6,7},{5,4},{7,6},{8,9},{10,11},{9,8... | collective-permute-start | bytes 12296 | tf_op jit(solution)/shard_map/ppermute | solution.py:211
  20.7 0.0 copy-done
  20.7 0.0 copy-done.1
  20.7 0.0 copy-done.2
  20.8 0.0 copy-done.4
  20.8 0.0 copy-done.5
  20.8 0.0 copy-done.6
  20.8 1.0 %local.1 = (f32[175,1024]{1,0:T(8,128)S(1)}, f32[375,1024]{1,0:T(8,128)S(1)}, f32[75,1024]{1,0:T(8,128)S(1)}, f32[75,1024]{1,0:T(8,128)S(1)}, bf16[175,320]{1,0:T(8,128)(2,1)S(1)}, /*index=5*/f32[1,1024]{1,0:T(1,128)S(1)}) custom-call(bf16[175,1024]{1,0:T(8,128)(2,1)S(1)} %get-tuple-element.33.tet_ref, bf16[375,1024]{1,0:T(8,128)(2,1)S(1)} %get-tuple-element.34.prism_ref, ...), custom_call_target="tpu_custom_call" | custom-call | flops 5000000000 | bytes 4000000 | tf_op jit(solution)/shard_map/local/pallas_call | solution.py:194
  21.8 0.0 collective-permute-done.1.from_odd_ref
  21.8 0.0 collective-permute-done.2.from_even_ref
  21.8 0.0 copy-start.3
  21.9 1.2 %tet_finish.1.tet_ref = bf16[175,1024]{1,0:T(8,128)(2,1)S(1)} custom-call(s32[1,1024]{1,0:T(1,128)S(1)} %get-tuple-element.28.code_ref, f32[1,1024]{1,0:T(1,128)S(1)} %get-tuple-element.43.live_ref, bf16[80,512]{1,0:T(8,128)(2,1)S(1)} %get-tuple-element.45.odd_ref, bf16[80,512]{1,0:T(8,128)(2,1)S(1)} %get-tuple-element.46.even_ref, ...), custom_call_target="tpu_custom_call" | custom-call | flops 5000000000 | bytes 3000000 | tf_op jit(solution)/shard_map/tet_finish/pallas_call | solution.py:194
  23.0 0.0 collective-permute-done.3.other_ref
  23.0 0.0 copy-done.3
  23.1 1.2 %prism_finish.1 = (bf16[175,1024]{1,0:T(8,128)(2,1)}, bf16[375,1024]{1,0:T(8,128)(2,1)}) custom-call(bf16[175,1024]{1,0:T(8,128)(2,1)S(1)} %tet_finish.1.tet_ref, f32[8,128]{1,0:T(8,128)S(1)} %add.3.pair_ref, f32[8,128]{1,0:T(8,128)S(1)} %collective-permute-done.3.other_ref, f32[1,4,6]{2,1,0:T(4,128)S(1)} %copy-done.5, ...), custom_call_target="tpu_custom_call" | custom-call | flops 5000000000 | bytes 3000000 | tf_op jit(solution)/shard_map/prism_finish/pallas_call | solution.py:194
  (1 shorter events, 0.0 us)
Async XLA Ops:
  2.2 9.2 %collective-permute-start = (f32[8,128]{1,0:T(8,128)S(1)}, f32[8,128]{1,0:T(8,128)S(1)}, u32[]{:S(2)}, u32[]{:S(2)}) collective-permute-start(f32[8,128]{1,0:T(8,128)S(1)} %get-tuple-element.30), channel_id=1, source_target_pairs={{0,3},{1,2},{3,0},{2,1},{4,7},{5,6},{7,4},{6,5},{8,11},{9,10},{11,... | collective-permute-start | bytes 12296 | tf_op jit(solution)/shard_map/ppermute | solution.py:211
  4.3 16.4 %copy-start = (bf16[375,375]{1,0:T(8,128)(2,1)S(1)}, bf16[375,375]{1,0:T(8,128)(2,1)}, u32[]{:S(2)}) copy-start(bf16[375,375]{1,0:T(8,128)(2,1)} %prism_volume_ref) | copy-start | bytes 843754
  4.4 16.4 %copy-start.1 = (bf16[175,300]{1,0:T(8,128)(2,1)S(1)}, bf16[175,300]{1,0:T(8,128)(2,1)}, u32[]{:S(2)}) copy-start(bf16[175,300]{1,0:T(8,128)(2,1)} %lift_ref) | copy-start | bytes 315004
  4.4 16.4 %copy-start.2 = (bf16[175,175]{1,0:T(8,128)(2,1)S(1)}, bf16[175,175]{1,0:T(8,128)(2,1)}, u32[]{:S(2)}) copy-start(bf16[175,175]{1,0:T(8,128)(2,1)} %volume_ref) | copy-start | bytes 183754
  4.4 16.4 %copy-start.4 = (f32[1024]{0:T(1024)S(1)}, f32[1024]{0:T(1024)}, u32[]{:S(2)}) copy-start(f32[1024]{0:T(1024)} %param.24) | copy-start | bytes 12292
  4.4 16.4 %copy-start.5 = (f32[1,4,6]{2,1,0:T(4,128)S(1)}, f32[1,4,6]{2,1,0:T(4,128)}, u32[]{:S(2)}) copy-start(f32[1,4,6]{2,1,0:T(4,128)} %law_ref.1) | copy-start | bytes 292
  4.4 16.4 %copy-start.6 = (s32[1,2]{1,0:T(1,128)S(1)}, s32[1,2]{1,0:T(1,128)}, u32[]{:S(2)}) copy-start(s32[1,2]{1,0:T(1,128)} %count_ref) | copy-start | bytes 28
  5.4 16.5 %collective-permute-start.1 = (bf16[80,512]{1,0:T(8,128)(2,1)S(1)}, bf16[80,512]{1,0:T(8,128)(2,1)S(1)}, u32[]{:S(2)}, u32[]{:S(2)}) collective-permute-start(bf16[80,512]{1,0:T(8,128)(2,1)S(1)} %get-tuple-element.45.odd_ref), channel_id=1, source_target_pairs={{4,8},{12,16},{20,24},{28,32},{36,40},{44,48},{52,56},{60,64},{68,... | collective-permute-start | bytes 245768 | tf_op jit(solution)/shard_map/ppermute | solution.py:211
  9.4 12.4 %collective-permute-start.2 = (bf16[80,512]{1,0:T(8,128)(2,1)S(1)}, bf16[80,512]{1,0:T(8,128)(2,1)S(1)}, u32[]{:S(2)}, u32[]{:S(2)}) collective-permute-start(bf16[80,512]{1,0:T(8,128)(2,1)S(1)} %get-tuple-element.46.even_ref), channel_id=1, source_target_pairs={{0,4},{8,12},{16,20},{24,28},{32,36},{40,44},{48,52},{56,60},{64,6... | collective-permute-start | bytes 245768 | tf_op jit(solution)/shard_map/ppermute | solution.py:211
  11.4 11.7 %collective-permute-start.3 = (f32[8,128]{1,0:T(8,128)S(1)}, f32[8,128]{1,0:T(8,128)S(1)}, u32[]{:S(2)}, u32[]{:S(2)}) collective-permute-start(f32[8,128]{1,0:T(8,128)S(1)} %add.3.pair_ref), channel_id=1, source_target_pairs={{0,1},{2,3},{1,0},{3,2},{4,5},{6,7},{5,4},{7,6},{8,9},{10,11},{9,8... | collective-permute-start | bytes 12296 | tf_op jit(solution)/shard_map/ppermute | solution.py:211
  21.8 1.2 %copy-start.3 = (bf16[375,75]{0,1:T(8,128)(2,1)S(1)}, bf16[375,75]{0,1:T(8,128)(2,1)}, u32[]{:S(2)}) copy-start(bf16[375,75]{0,1:T(8,128)(2,1)} %param.21) | copy-start | bytes 168754

commit v6 on v5

--- a/solution.py
+++ b/solution.py
@@ -95,7 +95,12 @@
         copy.wait()
 
 
-def face_kernel(code_ref, tet_ref, extrap_ref, odd_ref, even_ref):
+def early():
+    axial = lax.axis_index("axial")
+    return (axial < 2) & (axial + lax.axis_index("azim") > 0)
+
+
+def make_faces(code_ref, tet_ref, extrap_ref, odd_ref, even_ref):
     capacity = odd_ref.shape[1]
     pad = mm(spread(4 * FP, 4 * FW), extrap_ref[...], NT).astype(BF)
     left = faces_of(code_ref[...], tet_ref[...], pad)
@@ -104,7 +109,7 @@
     even_ref[...] = jnp.where(upper, left[:, capacity:], left[:, :capacity])
 
 
-def local_kernel(
+def make_local(
     tet_ref, prism_ref, wall_ref, owned_ref, volume_ref, prism_volume_ref, lift_ref, law_ref, count_ref, area_ref,
     tet_part_ref, prism_part_ref, rows_ref, gain_ref, pad_ref, live_ref,
 ):
@@ -136,6 +141,49 @@
         live_ref[:, side * capacity : (side + 1) * capacity] = jnp.where(slot < count_ref[:, side : side + 1], area, 0.0)
 
 
+def early_kernel(
+    code_ref, extrap_ref, tet_ref, prism_ref, wall_ref, owned_ref,
+    volume_hbm, prism_volume_hbm, lift_hbm, law_hbm, count_hbm, area_hbm,
+    odd_ref, even_ref, tet_part_ref, prism_part_ref, rows_ref, gain_ref, pad_ref, live_ref,
+    volume_ref, prism_volume_ref, lift_ref, law_ref, count_ref, area_ref, sems,
+):
+    @pl.when(early())
+    def _():
+        pairs = (
+            (volume_hbm, volume_ref), (prism_volume_hbm, prism_volume_ref), (lift_hbm, lift_ref),
+            (law_hbm, law_ref), (count_hbm, count_ref), (area_hbm, area_ref),
+        )
+        copies = [pltpu.make_async_copy(a, b, sems.at[n]) for n, (a, b) in enumerate(pairs)]
+        for copy in copies:
+            copy.start()
+        make_faces(code_ref, tet_ref, extrap_ref, odd_ref, even_ref)
+        for copy in copies:
+            copy.wait()
+        make_local(
+            tet_ref, prism_ref, wall_ref, owned_ref, volume_ref, prism_volume_ref, lift_ref, law_ref, count_ref, area_ref,
+            tet_part_ref, prism_part_ref, rows_ref, gain_ref, pad_ref, live_ref,
+        )
+
+
+def face_kernel(code_ref, tet_ref, extrap_ref, odd_in, even_in, odd_ref, even_ref):
+    @pl.when(jnp.logical_not(early()))
+    def _():
+        make_faces(code_ref, tet_ref, extrap_ref, odd_ref, even_ref)
+
+
+def local_kernel(
+    tet_ref, prism_ref, wall_ref, owned_ref, volume_ref, prism_volume_ref, lift_ref, law_ref, count_ref, area_ref,
+    tet_part_in, prism_part_in, rows_in, gain_in, pad_in, live_in,
+    tet_part_ref, prism_part_ref, rows_ref, gain_ref, pad_ref, live_ref,
+):
+    @pl.when(jnp.logical_not(early()))
+    def _():
+        make_local(
+            tet_ref, prism_ref, wall_ref, owned_ref, volume_ref, prism_volume_ref, lift_ref, law_ref, count_ref, area_ref,
+            tet_part_ref, prism_part_ref, rows_ref, gain_ref, pad_ref, live_ref,
+        )
+
+
 def tet_kernel(code_ref, live_ref, odd_ref, even_ref, from_odd_ref, from_even_ref, part_ref, pad_ref, out_ref):
     first = first_side()
     capacity = even_ref.shape[1]
@@ -190,13 +238,14 @@
 HB = pl.BlockSpec(memory_space=pltpu.HBM)
 
 
-def call(kernel, name, outs, out_specs, specs, flops, moved, args, scratch=()):
+def call(kernel, name, outs, out_specs, specs, flops, moved, args, scratch=(), aliases=()):
     return pl.pallas_call(
         kernel,
         out_shape=outs,
         in_specs=specs,
         out_specs=out_specs,
         scratch_shapes=scratch,
+        input_output_aliases=dict(aliases),
         cost_estimate=pl.CostEstimate(flops=flops, bytes_accessed=moved, transcendentals=0),
         compiler_params=pltpu.CompilerParams(vmem_limit_bytes=32 * 1024 * 1024),
         name=name,
@@ -250,8 +299,30 @@
         tuple(hbm(x, pltpu.HBM) for x in operands),
         [like(x) for x in operands[:2]] + [pltpu.SemaphoreType.DMA((7,))],
     )
+    local_outs = (
+        pltpu.VMEM(tet.shape, F32),
+        pltpu.VMEM(prism.shape, F32),
+        pltpu.VMEM((FW, tall), F32),
+        pltpu.VMEM((FW, tall), F32),
+        pltpu.VMEM((tet.shape[0], 4 * FP), BF),
+        like(area),
+    )
+    operands = (tet_volume, prism_volume, face_lift, burn_law, face_count, area)
+    odd, even, *made = call(
+        early_kernel,
+        "early",
+        (side, side) + local_outs,
+        (VM,) * 8,
+        [VM] * 6 + [HB] * 6,
+        5_000_000_000,
+        3_000_000,
+        (code, extrap, tet, prism, wall, owned) + tuple(hbm(x, pltpu.HBM) for x in operands),
+        [like(x) for x in operands] + [pltpu.SemaphoreType.DMA((6,))],
+    )
+    part, odd, even, *made = lax.optimization_barrier((part, odd, even, *made))
     odd, even = call(
-        face_kernel, "faces", (side, side), (VM, VM), [VM] * 3, 5_000_000_000, 600_000, (code, tet, extrap)
+        face_kernel, "faces", (side, side), (VM, VM), [VM] * 5, 5_000_000_000, 600_000, (code, tet, extrap, odd, even),
+        aliases=((3, 0), (4, 1)),
     )
     part, tet_volume, prism_volume, face_lift, wall_lift, law, face_count, area = lax.optimization_barrier(
         (part, tet_volume, prism_volume, face_lift, wall_lift, burn_law, face_count, area)
@@ -266,19 +337,13 @@
     tet_part, prism_part, rows, gain, pad, live = call(
         local_kernel,
         "local",
-        (
-            pltpu.VMEM(tet.shape, F32),
-            pltpu.VMEM(prism.shape, F32),
-            pltpu.VMEM((FW, tall), F32),
-            pltpu.VMEM((FW, tall), F32),
-            pltpu.VMEM((tet.shape[0], 4 * FP), BF),
-            like(area),
-        ),
+        local_outs,
         (VM,) * 6,
-        [VM] * 10,
+        [VM] * 16,
         5_000_000_000,
         4_000_000,
-        (tet, prism, wall, owned, tet_volume, prism_volume, face_lift, law, face_count, area),
+        (tet, prism, wall, owned, tet_volume, prism_volume, face_lift, law, face_count, area, *made),
+        aliases=tuple((10 + n, n) for n in range(6)),
     )
     tet_new = call(
         tet_kernel,

time: 24.5 us -> 24.3 us (level)
  the two profiles are of different devices: /device:TPU:5 before, /device:TPU:1 now
where the time goes in v6:
time: 24.3 us; the launch traced here: 24.1 us
  starting transfers between devices  15.9 us (65%)
  Pallas kernels  6.21 us (26%)
  waiting for transfers between devices  1.12 us (5%)
  between operations  0.84 us (3%)
    ppermute x4, starting transfers between devices, swap(): return lax.ppermute(value, axis, list(pairs) + [(j, i) for i, j in pairs])  15.9 us
    pallas_call x6, Pallas kernels, call(): pl.pallas_call(kernel, out_shape=outs, in_specs=specs, out_specs=out_spec...  6.21 us
    ppermute x4, waiting for transfers between devices, swap(): return lax.ppermute(value, axis, list(pairs) + [(j, i) for i, j in pairs])  1.12 us
  transfers between devices with their start and end apart: 4, of which 1 were waited for; matrix products, arithmetic and copies ran while one was open for 0% of the time, Pallas kernels for 5%

profile of v6, /device:TPU:1, one launch (start us, length us, event | category | flops | bytes accessed | tf_op | source)
XLA Modules:
  0.0 24.1 jit_solution(5442888577498298863)
XLA Ops:
  0.6 1.5 %walls.1 = (f32[8,128]{1,0:T(8,128)S(1)}, f32[8,1024]{1,0:T(8,128)S(1)}, bf16[375,1024]{1,0:T(8,128)(2,1)S(1)}, bf16[75,375]{1,0:T(8,128)(2,1)S(1)}, bf16[175,10...) custom-call(s32[1,512]{1,0:T(1,128)} %bitcast.11, s32[1,512]{1,0:T(1,128)} %bitcast.12, ...), custom_call_target="tpu_custom_call" | custom-call | flops 5000000000 | bytes 3000000 | tf_op jit(solution)/shard_map/walls/pallas_call | solution.py:242
  2.2 2.2 %early.1 = (bf16[80,512]{1,0:T(8,128)(2,1)S(1)}, bf16[80,512]{1,0:T(8,128)(2,1)S(1)}, f32[175,1024]{1,0:T(8,128)S(1)}, f32[375,1024]{1,0:T(8,128)S(1)}, f32[75,1...) custom-call(s32[1,1024]{1,0:T(1,128)S(1)} %get-tuple-element.45.code_ref, ...), custom_call_target="tpu_custom_call" | custom-call | flops 5000000000 | bytes 3000000 | tf_op jit(solution)/shard_map/early/pallas_call | solution.py:242
  4.4 0.0 copy-start
  4.4 0.0 copy-start.1
  4.4 0.0 copy-start.2
  4.4 0.0 copy-start.4
  4.4 0.0 copy-start.5
  4.4 0.0 copy-start.6
  4.5 5.3 %collective-permute-start = (f32[8,128]{1,0:T(8,128)S(1)}, f32[8,128]{1,0:T(8,128)S(1)}, u32[]{:S(2)}, u32[]{:S(2)}) collective-permute-start(f32[8,128]{1,0:T(8,128)S(1)} %get-tuple-element.61), channel_id=1, source_target_pairs={{0,3},{1,2},{3,0},{2,1},{4,7},{5,6},{7,4},{6,5},{8,11},{9,10},{11,... | collective-permute-start | bytes 12296 | tf_op jit(solution)/shard_map/ppermute | solution.py:260
  9.8 2.9 %collective-permute-start.1 = (bf16[80,512]{1,0:T(8,128)(2,1)S(1)}, bf16[80,512]{1,0:T(8,128)(2,1)S(1)}, u32[]{:S(2)}, u32[]{:S(2)}) collective-permute-start(bf16[80,512]{1,0:T(8,128)(2,1)S(1)} %get-tuple-element.79.odd_ref), channel_id=1, source_target_pairs={{4,8},{12,16},{20,24},{28,32},{36,40},{44,48},{52,56},{60,64},{68,... | collective-permute-start | bytes 245768 | tf_op jit(solution)/shard_map/ppermute | solution.py:260
  12.7 5.7 %collective-permute-start.2 = (bf16[80,512]{1,0:T(8,128)(2,1)S(1)}, bf16[80,512]{1,0:T(8,128)(2,1)S(1)}, u32[]{:S(2)}, u32[]{:S(2)}) collective-permute-start(bf16[80,512]{1,0:T(8,128)(2,1)S(1)} %get-tuple-element.80.even_ref), channel_id=1, source_target_pairs={{0,4},{8,12},{16,20},{24,28},{32,36},{40,44},{48,52},{56,60},{64,6... | collective-permute-start | bytes 245768 | tf_op jit(solution)/shard_map/ppermute | solution.py:260
  18.5 0.0 collective-permute-done
  18.5 1.9 %collective-permute-start.3 = (f32[8,128]{1,0:T(8,128)S(1)}, f32[8,128]{1,0:T(8,128)S(1)}, u32[]{:S(2)}, u32[]{:S(2)}) collective-permute-start(f32[8,128]{1,0:T(8,128)S(1)} %add.3.pair_ref), channel_id=1, source_target_pairs={{0,1},{2,3},{1,0},{3,2},{4,5},{6,7},{5,4},{7,6},{8,9},{10,11},{9,8... | collective-permute-start | bytes 12296 | tf_op jit(solution)/shard_map/ppermute | solution.py:260
  20.4 0.0 copy-done
  20.4 0.0 copy-done.1
  20.4 0.0 copy-done.2
  20.4 0.0 copy-done.4
  20.5 0.0 copy-done.5
  20.5 0.0 copy-done.6
  20.5 0.0 collective-permute-done.1.from_odd_ref
  20.5 0.0 collective-permute-done.2.from_even_ref
  20.5 0.0 copy-start.3
  20.5 1.2 %tet_finish.1.tet_ref = bf16[175,1024]{1,0:T(8,128)(2,1)S(1)} custom-call(s32[1,1024]{1,0:T(1,128)S(1)} %get-tuple-element.45.code_ref, f32[1,1024]{1,0:T(1,128)S(1)} %get-tuple-element.76.live_ref, bf16[80,512]{1,0:T(8,128)(2,1)S(1)} %get-tuple-element.79.odd_ref, bf16[80,512]{1,0:T(8,128)(2,1)S(1)} %get-tuple-element.80.even_ref, ...), custom_call_target="tpu_custom_call" | custom-call | flops 5000000000 | bytes 3000000 | tf_op jit(solution)/shard_map/tet_finish/pallas_call | solution.py:242
  21.7 1.1 %collective-permute-done.3.other_ref = f32[8,128]{1,0:T(8,128)S(1)} collective-permute-done((f32[8,128]{1,0:T(8,128)S(1)}, f32[8,128]{1,0:T(8,128)S(1)}, u32[]{:S(2)}, u32[]{:S(2)}) %collective-permute-start.3) | collective-permute-done | bytes 4128 | tf_op jit(solution)/shard_map/ppermute | solution.py:260
  22.8 0.0 copy-done.3
  22.8 1.2 %prism_finish.1 = (bf16[175,1024]{1,0:T(8,128)(2,1)}, bf16[375,1024]{1,0:T(8,128)(2,1)}) custom-call(bf16[175,1024]{1,0:T(8,128)(2,1)S(1)} %tet_finish.1.tet_ref, f32[8,128]{1,0:T(8,128)S(1)} %add.3.pair_ref, f32[8,128]{1,0:T(8,128)S(1)} %collective-permute-done.3.other_ref, f32[1,4,6]{2,1,0:T(4,128)S(1)} %copy-done.5, ...), custom_call_target="tpu_custom_call" | custom-call | flops 5000000000 | bytes 3000000 | tf_op jit(solution)/shard_map/prism_finish/pallas_call | solution.py:242
  (3 shorter events, 0.1 us)
Async XLA Ops:
  4.4 16.0 %copy-start = (bf16[375,375]{1,0:T(8,128)(2,1)S(1)}, bf16[375,375]{1,0:T(8,128)(2,1)}, u32[]{:S(2)}) copy-start(bf16[375,375]{1,0:T(8,128)(2,1)} %prism_volume_ref) | copy-start | bytes 843754
  4.4 16.0 %copy-start.1 = (bf16[175,300]{1,0:T(8,128)(2,1)S(1)}, bf16[175,300]{1,0:T(8,128)(2,1)}, u32[]{:S(2)}) copy-start(bf16[175,300]{1,0:T(8,128)(2,1)} %lift_ref) | copy-start | bytes 315004
  4.4 16.0 %copy-start.2 = (bf16[175,175]{1,0:T(8,128)(2,1)S(1)}, bf16[175,175]{1,0:T(8,128)(2,1)}, u32[]{:S(2)}) copy-start(bf16[175,175]{1,0:T(8,128)(2,1)} %volume_ref) | copy-start | bytes 183754
  4.4 16.0 %copy-start.4 = (f32[1024]{0:T(1024)S(1)}, f32[1024]{0:T(1024)}, u32[]{:S(2)}) copy-start(f32[1024]{0:T(1024)} %param.24) | copy-start | bytes 12292
  4.4 16.0 %copy-start.5 = (f32[1,4,6]{2,1,0:T(4,128)S(1)}, f32[1,4,6]{2,1,0:T(4,128)}, u32[]{:S(2)}) copy-start(f32[1,4,6]{2,1,0:T(4,128)} %law_ref.1) | copy-start | bytes 292
  4.4 16.0 %copy-start.6 = (s32[1,2]{1,0:T(1,128)S(1)}, s32[1,2]{1,0:T(1,128)}, u32[]{:S(2)}) copy-start(s32[1,2]{1,0:T(1,128)} %count_ref) | copy-start | bytes 28
  4.5 14.0 %collective-permute-start = (f32[8,128]{1,0:T(8,128)S(1)}, f32[8,128]{1,0:T(8,128)S(1)}, u32[]{:S(2)}, u32[]{:S(2)}) collective-permute-start(f32[8,128]{1,0:T(8,128)S(1)} %get-tuple-element.61), channel_id=1, source_target_pairs={{0,3},{1,2},{3,0},{2,1},{4,7},{5,6},{7,4},{6,5},{8,11},{9,10},{11,... | collective-permute-start | bytes 12296 | tf_op jit(solution)/shard_map/ppermute | solution.py:260
  9.8 10.7 %collective-permute-start.1 = (bf16[80,512]{1,0:T(8,128)(2,1)S(1)}, bf16[80,512]{1,0:T(8,128)(2,1)S(1)}, u32[]{:S(2)}, u32[]{:S(2)}) collective-permute-start(bf16[80,512]{1,0:T(8,128)(2,1)S(1)} %get-tuple-element.79.odd_ref), channel_id=1, source_target_pairs={{4,8},{12,16},{20,24},{28,32},{36,40},{44,48},{52,56},{60,64},{68,... | collective-permute-start | bytes 245768 | tf_op jit(solution)/shard_map/ppermute | solution.py:260
  12.7 7.8 %collective-permute-start.2 = (bf16[80,512]{1,0:T(8,128)(2,1)S(1)}, bf16[80,512]{1,0:T(8,128)(2,1)S(1)}, u32[]{:S(2)}, u32[]{:S(2)}) collective-permute-start(bf16[80,512]{1,0:T(8,128)(2,1)S(1)} %get-tuple-element.80.even_ref), channel_id=1, source_target_pairs={{0,4},{8,12},{16,20},{24,28},{32,36},{40,44},{48,52},{56,60},{64,6... | collective-permute-start | bytes 245768 | tf_op jit(solution)/shard_map/ppermute | solution.py:260
  18.5 4.4 %collective-permute-start.3 = (f32[8,128]{1,0:T(8,128)S(1)}, f32[8,128]{1,0:T(8,128)S(1)}, u32[]{:S(2)}, u32[]{:S(2)}) collective-permute-start(f32[8,128]{1,0:T(8,128)S(1)} %add.3.pair_ref), channel_id=1, source_target_pairs={{0,1},{2,3},{1,0},{3,2},{4,5},{6,7},{5,4},{7,6},{8,9},{10,11},{9,8... | collective-permute-start | bytes 12296 | tf_op jit(solution)/shard_map/ppermute | solution.py:260
  20.5 2.3 %copy-start.3 = (bf16[375,75]{0,1:T(8,128)(2,1)S(1)}, bf16[375,75]{0,1:T(8,128)(2,1)}, u32[]{:S(2)}) copy-start(bf16[375,75]{0,1:T(8,128)(2,1)} %param.21) | copy-start | bytes 168754

commit v7 on v6

--- a/solution.py
+++ b/solution.py
@@ -66,33 +66,6 @@
 def side_of(ref, side):
     width = ref.shape[1] // 2
     return ref[:, pl.ds(pl.multiple_of(side * width, width), width)]
-
-
-def wall_kernel(
-    burn_hbm, owner_hbm, prism_hbm, wall_hbm, tet_hbm, code_hbm, extrap_hbm,
-    part_ref, owned_ref, prism_ref, wall_ref, tet_ref, code_ref, extrap_ref,
-    burn_ref, owner_ref, sems,
-):
-    pairs = (
-        (burn_hbm, burn_ref), (owner_hbm, owner_ref), (prism_hbm, prism_ref), (wall_hbm, wall_ref),
-        (tet_hbm, tet_ref), (code_hbm, code_ref), (extrap_hbm, extrap_ref),
-    )
-    copies = [pltpu.make_async_copy(a, b, sems.at[n]) for n, (a, b) in enumerate(pairs)]
-    for copy in copies:
-        copy.start()
-    for copy in copies[:2]:
-        copy.wait()
-    walls = burn_ref.shape[1]
-    place = hot(rows_of((prism_ref.shape[1], walls)) == burn_ref[...])
-    owned = mm(hot(rows_of((8, walls)) == owner_ref[...]), place, NT)
-    owned_ref[...] = owned
-    for copy in copies[2:4]:
-        copy.wait()
-    rows = mm(wall_ref[(NV - 1) * TFP : NV * TFP, :], prism_ref[...]).astype(BF).astype(F32)
-    sums = jnp.sum(rows * rows, axis=0, keepdims=True)
-    part_ref[...] = jnp.broadcast_to(jnp.sum(owned * sums, axis=1, keepdims=True), part_ref.shape)
-    for copy in copies[4:]:
-        copy.wait()
 
 
 def early():
@@ -141,23 +114,45 @@
         live_ref[:, side * capacity : (side + 1) * capacity] = jnp.where(slot < count_ref[:, side : side + 1], area, 0.0)
 
 
-def early_kernel(
-    code_ref, extrap_ref, tet_ref, prism_ref, wall_ref, owned_ref,
+def wall_kernel(
+    burn_hbm, owner_hbm, prism_hbm, wall_hbm, tet_hbm, code_hbm, extrap_hbm,
     volume_hbm, prism_volume_hbm, lift_hbm, law_hbm, count_hbm, area_hbm,
+    part_ref, owned_ref, prism_ref, wall_ref, tet_ref, code_ref, extrap_ref,
     odd_ref, even_ref, tet_part_ref, prism_part_ref, rows_ref, gain_ref, pad_ref, live_ref,
-    volume_ref, prism_volume_ref, lift_ref, law_ref, count_ref, area_ref, sems,
-):
+    burn_ref, owner_ref, volume_ref, prism_volume_ref, lift_ref, law_ref, count_ref, area_ref, sems,
+):
+    pairs = (
+        (burn_hbm, burn_ref), (owner_hbm, owner_ref), (prism_hbm, prism_ref), (wall_hbm, wall_ref),
+        (tet_hbm, tet_ref), (code_hbm, code_ref), (extrap_hbm, extrap_ref),
+    )
+    copies = [pltpu.make_async_copy(a, b, sems.at[n]) for n, (a, b) in enumerate(pairs)]
+    for copy in copies:
+        copy.start()
+    for copy in copies[:2]:
+        copy.wait()
+    walls = burn_ref.shape[1]
+    place = hot(rows_of((prism_ref.shape[1], walls)) == burn_ref[...])
+    owned = mm(hot(rows_of((8, walls)) == owner_ref[...]), place, NT)
+    owned_ref[...] = owned
+    for copy in copies[2:4]:
+        copy.wait()
+    rows = mm(wall_ref[(NV - 1) * TFP : NV * TFP, :], prism_ref[...]).astype(BF).astype(F32)
+    sums = jnp.sum(rows * rows, axis=0, keepdims=True)
+    part_ref[...] = jnp.broadcast_to(jnp.sum(owned * sums, axis=1, keepdims=True), part_ref.shape)
+    for copy in copies[4:]:
+        copy.wait()
+
     @pl.when(early())
     def _():
-        pairs = (
+        more = (
             (volume_hbm, volume_ref), (prism_volume_hbm, prism_volume_ref), (lift_hbm, lift_ref),
             (law_hbm, law_ref), (count_hbm, count_ref), (area_hbm, area_ref),
         )
-        copies = [pltpu.make_async_copy(a, b, sems.at[n]) for n, (a, b) in enumerate(pairs)]
-        for copy in copies:
+        late = [pltpu.make_async_copy(a, b, sems.at[len(pairs) + n]) for n, (a, b) in enumerate(more)]
+        for copy in late:
             copy.start()
         make_faces(code_ref, tet_ref, extrap_ref, odd_ref, even_ref)
-        for copy in copies:
+        for copy in late:
             copy.wait()
         make_local(
             tet_ref, prism_ref, wall_ref, owned_ref, volume_ref, prism_volume_ref, lift_ref, law_ref, count_ref, area_ref,
@@ -166,9 +161,18 @@
 
 
 def face_kernel(code_ref, tet_ref, extrap_ref, odd_in, even_in, odd_ref, even_ref):
-    @pl.when(jnp.logical_not(early()))
+    axial = lax.axis_index("axial")
+
+    @pl.when(jnp.logical_not(early()) & (axial > 0))
     def _():
         make_faces(code_ref, tet_ref, extrap_ref, odd_ref, even_ref)
+
+    @pl.when(jnp.logical_not(early()) & (axial == 0))
+    def _():
+        capacity = odd_ref.shape[1]
+        pad = mm(spread(4 * FP, 4 * FW), extrap_ref[...], NT).astype(BF)
+        odd_ref[...] = jnp.zeros_like(odd_ref)
+        even_ref[...] = faces_of(code_ref[:, capacity:], tet_ref[...], pad)
 
 
 def local_kernel(
@@ -288,38 +292,29 @@
     side = pltpu.VMEM((FP, capacity), BF)
     hbm = pltpu.with_memory_space_constraint
     operands = (burn, owner, prism_state, wall_extrap, tet_state, code, extrap)
-    part, owned, prism, wall, tet, code, extrap = call(
+    more = (tet_volume, prism_volume, face_lift, burn_law, face_count, area)
+    local_outs = (
+        pltpu.VMEM(tet_state.shape, F32),
+        pltpu.VMEM(prism_state.shape, F32),
+        pltpu.VMEM((FW, tall), F32),
+        pltpu.VMEM((FW, tall), F32),
+        pltpu.VMEM((tet_state.shape[0], 4 * FP), BF),
+        like(area),
+    )
+    part, owned, prism, wall, tet, code, extrap, odd, even, *made = call(
         wall_kernel,
         "walls",
-        (pltpu.VMEM((8, 128), F32), pltpu.VMEM((8, tall), F32)) + tuple(like(x) for x in operands[2:]),
-        (VM,) * 7,
-        [HB] * 7,
+        (pltpu.VMEM((8, 128), F32), pltpu.VMEM((8, tall), F32))
+        + tuple(like(x) for x in operands[2:])
+        + (side, side)
+        + local_outs,
+        (VM,) * 15,
+        [HB] * 13,
         5_000_000_000,
         3_000_000,
-        tuple(hbm(x, pltpu.HBM) for x in operands),
-        [like(x) for x in operands[:2]] + [pltpu.SemaphoreType.DMA((7,))],
-    )
-    local_outs = (
-        pltpu.VMEM(tet.shape, F32),
-        pltpu.VMEM(prism.shape, F32),
-        pltpu.VMEM((FW, tall), F32),
-        pltpu.VMEM((FW, tall), F32),
-        pltpu.VMEM((tet.shape[0], 4 * FP), BF),
-        like(area),
-    )
-    operands = (tet_volume, prism_volume, face_lift, burn_law, face_count, area)
-    odd, even, *made = call(
-        early_kernel,
-        "early",
-        (side, side) + local_outs,
-        (VM,) * 8,
-        [VM] * 6 + [HB] * 6,
-        5_000_000_000,
-        3_000_000,
-        (code, extrap, tet, prism, wall, owned) + tuple(hbm(x, pltpu.HBM) for x in operands),
-        [like(x) for x in operands] + [pltpu.SemaphoreType.DMA((6,))],
-    )
-    part, odd, even, *made = lax.optimization_barrier((part, odd, even, *made))
+        tuple(hbm(x, pltpu.HBM) for x in operands + more),
+        [like(x) for x in operands[:2] + more] + [pltpu.SemaphoreType.DMA((13,))],
+    )
     odd, even = call(
         face_kernel, "faces", (side, side), (VM, VM), [VM] * 5, 5_000_000_000, 600_000, (code, tet, extrap, odd, even),
         aliases=((3, 0), (4, 1)),

time: 24.3 us -> 24 us (0.988)
  starting transfers between devices: 15.9 us -> 15 us
  Pallas kernels: 6.21 us -> 6.79 us
    ppermute x4, starting transfers between devices: 15.9 us -> 15 us  [swap(): return lax.ppermute(value, axis, list(pairs) + [(j, i) for i, j in pairs])]
    pallas_call x6 -> x5, Pallas kernels: 6.21 us -> 6.79 us  [call(): pl.pallas_call(kernel, out_shape=outs, in_specs=specs, out_specs=out_spec...]
where the time goes in v7:
time: 24 us; the launch traced here: 23.8 us
  starting transfers between devices  15 us (62%)
  Pallas kernels  6.79 us (28%)
  waiting for transfers between devices  1.11 us (5%)
  between operations  0.83 us (3%)
    ppermute x4, starting transfers between devices, swap(): return lax.ppermute(value, axis, list(pairs) + [(j, i) for i, j in pairs])  15 us
    pallas_call x5, Pallas kernels, call(): pl.pallas_call(kernel, out_shape=outs, in_specs=specs, out_specs=out_spec...  6.79 us
    ppermute x4, waiting for transfers between devices, swap(): return lax.ppermute(value, axis, list(pairs) + [(j, i) for i, j in pairs])  1.11 us
  transfers between devices with their start and end apart: 4, of which 1 were waited for; matrix products, arithmetic and copies ran while one was open for 0% of the time, Pallas kernels for 5%

profile of v7, /device:TPU:1, one launch (start us, length us, event | category | flops | bytes accessed | tf_op | source)
XLA Modules:
  0.0 23.8 jit_solution(13037743415707966017)
XLA Ops:
  0.6 4.3 %walls.1 = (f32[8,128]{1,0:T(8,128)S(1)}, f32[8,1024]{1,0:T(8,128)S(1)}, bf16[375,1024]{1,0:T(8,128)(2,1)S(1)}, bf16[75,375]{1,0:T(8,128)(2,1)S(1)}, bf16[175,10...) custom-call(s32[1,512]{1,0:T(1,128)} %bitcast.11, ...), custom_call_target="tpu_custom_call" | custom-call | flops 5000000000 | bytes 3000000 | tf_op jit(solution)/shard_map/walls/pallas_call | solution.py:246
  4.9 5.2 %collective-permute-start = (f32[8,128]{1,0:T(8,128)S(1)}, f32[8,128]{1,0:T(8,128)S(1)}, u32[]{:S(2)}, u32[]{:S(2)}) collective-permute-start(f32[8,128]{1,0:T(8,128)S(1)} %get-tuple-element.38), channel_id=1, source_target_pairs={{0,3},{1,2},{3,0},{2,1},{4,7},{5,6},{7,4},{6,5},{8,11},{9,10},{11,... | collective-permute-start | bytes 12296 | tf_op jit(solution)/shard_map/ppermute | solution.py:264
  10.2 0.0 copy-start
  10.2 0.0 copy-start.1
  10.2 0.0 copy-start.2
  10.2 0.0 copy-start.4
  10.2 0.0 copy-start.5
  10.2 0.0 copy-start.6
  10.3 2.3 %collective-permute-start.1 = (bf16[80,512]{1,0:T(8,128)(2,1)S(1)}, bf16[80,512]{1,0:T(8,128)(2,1)S(1)}, u32[]{:S(2)}, u32[]{:S(2)}) collective-permute-start(bf16[80,512]{1,0:T(8,128)(2,1)S(1)} %get-tuple-element.61.odd_ref), channel_id=1, source_target_pairs={{4,8},{12,16},{20,24},{28,32},{36,40},{44,48},{52,56},{60,64},{68,... | collective-permute-start | bytes 245768 | tf_op jit(solution)/shard_map/ppermute | solution.py:264
  12.6 5.6 %collective-permute-start.2 = (bf16[80,512]{1,0:T(8,128)(2,1)S(1)}, bf16[80,512]{1,0:T(8,128)(2,1)S(1)}, u32[]{:S(2)}, u32[]{:S(2)}) collective-permute-start(bf16[80,512]{1,0:T(8,128)(2,1)S(1)} %get-tuple-element.62.even_ref), channel_id=1, source_target_pairs={{0,4},{8,12},{16,20},{24,28},{32,36},{40,44},{48,52},{56,60},{64,6... | collective-permute-start | bytes 245768 | tf_op jit(solution)/shard_map/ppermute | solution.py:264
  18.1 0.0 collective-permute-done
  18.2 1.9 %collective-permute-start.3 = (f32[8,128]{1,0:T(8,128)S(1)}, f32[8,128]{1,0:T(8,128)S(1)}, u32[]{:S(2)}, u32[]{:S(2)}) collective-permute-start(f32[8,128]{1,0:T(8,128)S(1)} %add.3.pair_ref), channel_id=1, source_target_pairs={{0,1},{2,3},{1,0},{3,2},{4,5},{6,7},{5,4},{7,6},{8,9},{10,11},{9,8... | collective-permute-start | bytes 12296 | tf_op jit(solution)/shard_map/ppermute | solution.py:264
  20.1 0.0 copy-done
  20.1 0.0 copy-done.1
  20.1 0.0 copy-done.2
  20.1 0.0 copy-done.4
  20.1 0.0 copy-done.5
  20.1 0.0 copy-done.6
  20.2 0.0 collective-permute-done.1.from_odd_ref
  20.2 0.0 collective-permute-done.2.from_even_ref
  20.2 0.0 copy-start.3
  20.2 1.2 %tet_finish.1.tet_ref = bf16[175,1024]{1,0:T(8,128)(2,1)S(1)} custom-call(s32[1,1024]{1,0:T(1,128)S(1)} %get-tuple-element.36.code_ref, f32[1,1024]{1,0:T(1,128)S(1)} %get-tuple-element.57.live_ref, bf16[80,512]{1,0:T(8,128)(2,1)S(1)} %get-tuple-element.61.odd_ref, bf16[80,512]{1,0:T(8,128)(2,1)S(1)} %get-tuple-element.62.even_ref, ...), custom_call_target="tpu_custom_call" | custom-call | flops 5000000000 | bytes 3000000 | tf_op jit(solution)/shard_map/tet_finish/pallas_call | solution.py:246
  21.4 1.1 %collective-permute-done.3.other_ref = f32[8,128]{1,0:T(8,128)S(1)} collective-permute-done((f32[8,128]{1,0:T(8,128)S(1)}, f32[8,128]{1,0:T(8,128)S(1)}, u32[]{:S(2)}, u32[]{:S(2)}) %collective-permute-start.3) | collective-permute-done | bytes 4128 | tf_op jit(solution)/shard_map/ppermute | solution.py:264
  22.5 0.0 copy-done.3
  22.5 1.2 %prism_finish.1 = (bf16[175,1024]{1,0:T(8,128)(2,1)}, bf16[375,1024]{1,0:T(8,128)(2,1)}) custom-call(bf16[175,1024]{1,0:T(8,128)(2,1)S(1)} %tet_finish.1.tet_ref, f32[8,128]{1,0:T(8,128)S(1)} %add.3.pair_ref, f32[8,128]{1,0:T(8,128)S(1)} %collective-permute-done.3.other_ref, f32[1,4,6]{2,1,0:T(4,128)S(1)} %copy-done.5, ...), custom_call_target="tpu_custom_call" | custom-call | flops 5000000000 | bytes 3000000 | tf_op jit(solution)/shard_map/prism_finish/pallas_call | solution.py:246
  (3 shorter events, 0.1 us)
Async XLA Ops:
  4.9 13.2 %collective-permute-start = (f32[8,128]{1,0:T(8,128)S(1)}, f32[8,128]{1,0:T(8,128)S(1)}, u32[]{:S(2)}, u32[]{:S(2)}) collective-permute-start(f32[8,128]{1,0:T(8,128)S(1)} %get-tuple-element.38), channel_id=1, source_target_pairs={{0,3},{1,2},{3,0},{2,1},{4,7},{5,6},{7,4},{6,5},{8,11},{9,10},{11,... | collective-permute-start | bytes 12296 | tf_op jit(solution)/shard_map/ppermute | solution.py:264
  10.2 9.9 %copy-start = (bf16[375,375]{1,0:T(8,128)(2,1)S(1)}, bf16[375,375]{1,0:T(8,128)(2,1)}, u32[]{:S(2)}) copy-start(bf16[375,375]{1,0:T(8,128)(2,1)} %prism_volume_ref) | copy-start | bytes 843754
  10.2 9.9 %copy-start.1 = (bf16[175,300]{1,0:T(8,128)(2,1)S(1)}, bf16[175,300]{1,0:T(8,128)(2,1)}, u32[]{:S(2)}) copy-start(bf16[175,300]{1,0:T(8,128)(2,1)} %lift_ref) | copy-start | bytes 315004
  10.2 9.9 %copy-start.2 = (bf16[175,175]{1,0:T(8,128)(2,1)S(1)}, bf16[175,175]{1,0:T(8,128)(2,1)}, u32[]{:S(2)}) copy-start(bf16[175,175]{1,0:T(8,128)(2,1)} %volume_ref) | copy-start | bytes 183754
  10.2 9.9 %copy-start.4 = (f32[1024]{0:T(1024)S(1)}, f32[1024]{0:T(1024)}, u32[]{:S(2)}) copy-start(f32[1024]{0:T(1024)} %param.24) | copy-start | bytes 12292
  10.2 9.9 %copy-start.5 = (f32[1,4,6]{2,1,0:T(4,128)S(1)}, f32[1,4,6]{2,1,0:T(4,128)}, u32[]{:S(2)}) copy-start(f32[1,4,6]{2,1,0:T(4,128)} %law_ref.1) | copy-start | bytes 292
  10.2 9.9 %copy-start.6 = (s32[1,2]{1,0:T(1,128)S(1)}, s32[1,2]{1,0:T(1,128)}, u32[]{:S(2)}) copy-start(s32[1,2]{1,0:T(1,128)} %count_ref) | copy-start | bytes 28
  10.3 9.9 %collective-permute-start.1 = (bf16[80,512]{1,0:T(8,128)(2,1)S(1)}, bf16[80,512]{1,0:T(8,128)(2,1)S(1)}, u32[]{:S(2)}, u32[]{:S(2)}) collective-permute-start(bf16[80,512]{1,0:T(8,128)(2,1)S(1)} %get-tuple-element.61.odd_ref), channel_id=1, source_target_pairs={{4,8},{12,16},{20,24},{28,32},{36,40},{44,48},{52,56},{60,64},{68,... | collective-permute-start | bytes 245768 | tf_op jit(solution)/shard_map/ppermute | solution.py:264
  12.6 7.6 %collective-permute-start.2 = (bf16[80,512]{1,0:T(8,128)(2,1)S(1)}, bf16[80,512]{1,0:T(8,128)(2,1)S(1)}, u32[]{:S(2)}, u32[]{:S(2)}) collective-permute-start(bf16[80,512]{1,0:T(8,128)(2,1)S(1)} %get-tuple-element.62.even_ref), channel_id=1, source_target_pairs={{0,4},{8,12},{16,20},{24,28},{32,36},{40,44},{48,52},{56,60},{64,6... | collective-permute-start | bytes 245768 | tf_op jit(solution)/shard_map/ppermute | solution.py:264
  18.2 4.4 %collective-permute-start.3 = (f32[8,128]{1,0:T(8,128)S(1)}, f32[8,128]{1,0:T(8,128)S(1)}, u32[]{:S(2)}, u32[]{:S(2)}) collective-permute-start(f32[8,128]{1,0:T(8,128)S(1)} %add.3.pair_ref), channel_id=1, source_target_pairs={{0,1},{2,3},{1,0},{3,2},{4,5},{6,7},{5,4},{7,6},{8,9},{10,11},{9,8... | collective-permute-start | bytes 12296 | tf_op jit(solution)/shard_map/ppermute | solution.py:264
  20.2 2.3 %copy-start.3 = (bf16[375,75]{0,1:T(8,128)(2,1)S(1)}, bf16[375,75]{0,1:T(8,128)(2,1)}, u32[]{:S(2)}) copy-start(bf16[375,75]{0,1:T(8,128)(2,1)} %param.21) | copy-start | bytes 168754

commit v8 on v7

--- a/solution.py
+++ b/solution.py
@@ -219,10 +219,10 @@
     sums = (pair_ref[...] + other_ref[...])[:SECTORS]
     damping = 1.0 / (1.0 + law_ref[0, :, 0:1] * sums / (BW_DEV * TFP))
     elements = part_ref.shape[1]
-    width = elements // 4
+    width = elements // 8
     lift = lift_ref[...]
     outs = []
-    for n in range(4):
+    for n in range(8):
         at = slice(n * width, (n + 1) * width)
         factor = jnp.zeros((1, width), F32)
         for o in range(SECTORS):
@@ -359,7 +359,7 @@
         5_000_000_000,
         3_000_000,
         (tet_new, pair, other, law, owned, rows, gain, prism_part, wall_lift),
-        [like(prism), pltpu.SemaphoreType.DMA((5,))],
+        [like(prism), pltpu.SemaphoreType.DMA((9,))],
     )
     return (tet_new, prism_new)
 

time: 24 us -> 24 us (level)
  no operation moved by 1% of the time
where the time goes in v8:
time: 24 us; the launch traced here: 23.8 us
  starting transfers between devices  15 us (62%)
  Pallas kernels  6.81 us (28%)
  waiting for transfers between devices  1.11 us (5%)
  between operations  0.83 us (3%)
    ppermute x4, starting transfers between devices, swap(): return lax.ppermute(value, axis, list(pairs) + [(j, i) for i, j in pairs])  15 us
    pallas_call x5, Pallas kernels, call(): pl.pallas_call(kernel, out_shape=outs, in_specs=specs, out_specs=out_spec...  6.81 us
    ppermute x4, waiting for transfers between devices, swap(): return lax.ppermute(value, axis, list(pairs) + [(j, i) for i, j in pairs])  1.11 us
  transfers between devices with their start and end apart: 4, of which 1 were waited for; matrix products, arithmetic and copies ran while one was open for 0% of the time, Pallas kernels for 5%

profile of v8, /device:TPU:1, one launch (start us, length us, event | category | flops | bytes accessed | tf_op | source)
XLA Modules:
  0.0 23.8 jit_solution(6539434686138777934)
XLA Ops:
  0.6 4.3 %walls.1 = (f32[8,128]{1,0:T(8,128)S(1)}, f32[8,1024]{1,0:T(8,128)S(1)}, bf16[375,1024]{1,0:T(8,128)(2,1)S(1)}, bf16[75,375]{1,0:T(8,128)(2,1)S(1)}, bf16[175,10...) custom-call(s32[1,512]{1,0:T(1,128)} %bitcast.11, ...), custom_call_target="tpu_custom_call" | custom-call | flops 5000000000 | bytes 3000000 | tf_op jit(solution)/shard_map/walls/pallas_call | solution.py:246
  4.9 5.2 %collective-permute-start = (f32[8,128]{1,0:T(8,128)S(1)}, f32[8,128]{1,0:T(8,128)S(1)}, u32[]{:S(2)}, u32[]{:S(2)}) collective-permute-start(f32[8,128]{1,0:T(8,128)S(1)} %get-tuple-element.38), channel_id=1, source_target_pairs={{0,3},{1,2},{3,0},{2,1},{4,7},{5,6},{7,4},{6,5},{8,11},{9,10},{11,... | collective-permute-start | bytes 12296 | tf_op jit(solution)/shard_map/ppermute | solution.py:264
  10.2 0.0 copy-start
  10.2 0.0 copy-start.1
  10.2 0.0 copy-start.2
  10.2 0.0 copy-start.4
  10.2 0.0 copy-start.5
  10.2 0.0 copy-start.6
  10.3 2.3 %collective-permute-start.1 = (bf16[80,512]{1,0:T(8,128)(2,1)S(1)}, bf16[80,512]{1,0:T(8,128)(2,1)S(1)}, u32[]{:S(2)}, u32[]{:S(2)}) collective-permute-start(bf16[80,512]{1,0:T(8,128)(2,1)S(1)} %get-tuple-element.61.odd_ref), channel_id=1, source_target_pairs={{4,8},{12,16},{20,24},{28,32},{36,40},{44,48},{52,56},{60,64},{68,... | collective-permute-start | bytes 245768 | tf_op jit(solution)/shard_map/ppermute | solution.py:264
  12.6 5.6 %collective-permute-start.2 = (bf16[80,512]{1,0:T(8,128)(2,1)S(1)}, bf16[80,512]{1,0:T(8,128)(2,1)S(1)}, u32[]{:S(2)}, u32[]{:S(2)}) collective-permute-start(bf16[80,512]{1,0:T(8,128)(2,1)S(1)} %get-tuple-element.62.even_ref), channel_id=1, source_target_pairs={{0,4},{8,12},{16,20},{24,28},{32,36},{40,44},{48,52},{56,60},{64,6... | collective-permute-start | bytes 245768 | tf_op jit(solution)/shard_map/ppermute | solution.py:264
  18.1 0.0 collective-permute-done
  18.2 1.9 %collective-permute-start.3 = (f32[8,128]{1,0:T(8,128)S(1)}, f32[8,128]{1,0:T(8,128)S(1)}, u32[]{:S(2)}, u32[]{:S(2)}) collective-permute-start(f32[8,128]{1,0:T(8,128)S(1)} %add.3.pair_ref), channel_id=1, source_target_pairs={{0,1},{2,3},{1,0},{3,2},{4,5},{6,7},{5,4},{7,6},{8,9},{10,11},{9,8... | collective-permute-start | bytes 12296 | tf_op jit(solution)/shard_map/ppermute | solution.py:264
  20.1 0.0 copy-done
  20.1 0.0 copy-done.1
  20.1 0.0 copy-done.2
  20.1 0.0 copy-done.4
  20.1 0.0 copy-done.5
  20.1 0.0 copy-done.6
  20.2 0.0 collective-permute-done.1.from_odd_ref
  20.2 0.0 collective-permute-done.2.from_even_ref
  20.2 0.0 copy-start.3
  20.2 1.2 %tet_finish.1.tet_ref = bf16[175,1024]{1,0:T(8,128)(2,1)S(1)} custom-call(s32[1,1024]{1,0:T(1,128)S(1)} %get-tuple-element.36.code_ref, f32[1,1024]{1,0:T(1,128)S(1)} %get-tuple-element.57.live_ref, bf16[80,512]{1,0:T(8,128)(2,1)S(1)} %get-tuple-element.61.odd_ref, bf16[80,512]{1,0:T(8,128)(2,1)S(1)} %get-tuple-element.62.even_ref, ...), custom_call_target="tpu_custom_call" | custom-call | flops 5000000000 | bytes 3000000 | tf_op jit(solution)/shard_map/tet_finish/pallas_call | solution.py:246
  21.4 1.1 %collective-permute-done.3.other_ref = f32[8,128]{1,0:T(8,128)S(1)} collective-permute-done((f32[8,128]{1,0:T(8,128)S(1)}, f32[8,128]{1,0:T(8,128)S(1)}, u32[]{:S(2)}, u32[]{:S(2)}) %collective-permute-start.3) | collective-permute-done | bytes 4128 | tf_op jit(solution)/shard_map/ppermute | solution.py:264
  22.5 0.0 copy-done.3
  22.5 1.3 %prism_finish.1 = (bf16[175,1024]{1,0:T(8,128)(2,1)}, bf16[375,1024]{1,0:T(8,128)(2,1)}) custom-call(bf16[175,1024]{1,0:T(8,128)(2,1)S(1)} %tet_finish.1.tet_ref, f32[8,128]{1,0:T(8,128)S(1)} %add.3.pair_ref, f32[8,128]{1,0:T(8,128)S(1)} %collective-permute-done.3.other_ref, f32[1,4,6]{2,1,0:T(4,128)S(1)} %copy-done.5, ...), custom_call_target="tpu_custom_call" | custom-call | flops 5000000000 | bytes 3000000 | tf_op jit(solution)/shard_map/prism_finish/pallas_call | solution.py:246
  (3 shorter events, 0.1 us)
Async XLA Ops:
  4.9 13.2 %collective-permute-start = (f32[8,128]{1,0:T(8,128)S(1)}, f32[8,128]{1,0:T(8,128)S(1)}, u32[]{:S(2)}, u32[]{:S(2)}) collective-permute-start(f32[8,128]{1,0:T(8,128)S(1)} %get-tuple-element.38), channel_id=1, source_target_pairs={{0,3},{1,2},{3,0},{2,1},{4,7},{5,6},{7,4},{6,5},{8,11},{9,10},{11,... | collective-permute-start | bytes 12296 | tf_op jit(solution)/shard_map/ppermute | solution.py:264
  10.2 9.9 %copy-start = (bf16[375,375]{1,0:T(8,128)(2,1)S(1)}, bf16[375,375]{1,0:T(8,128)(2,1)}, u32[]{:S(2)}) copy-start(bf16[375,375]{1,0:T(8,128)(2,1)} %prism_volume_ref) | copy-start | bytes 843754
  10.2 9.9 %copy-start.1 = (bf16[175,300]{1,0:T(8,128)(2,1)S(1)}, bf16[175,300]{1,0:T(8,128)(2,1)}, u32[]{:S(2)}) copy-start(bf16[175,300]{1,0:T(8,128)(2,1)} %lift_ref) | copy-start | bytes 315004
  10.2 9.9 %copy-start.2 = (bf16[175,175]{1,0:T(8,128)(2,1)S(1)}, bf16[175,175]{1,0:T(8,128)(2,1)}, u32[]{:S(2)}) copy-start(bf16[175,175]{1,0:T(8,128)(2,1)} %volume_ref) | copy-start | bytes 183754
  10.2 9.9 %copy-start.4 = (f32[1024]{0:T(1024)S(1)}, f32[1024]{0:T(1024)}, u32[]{:S(2)}) copy-start(f32[1024]{0:T(1024)} %param.24) | copy-start | bytes 12292
  10.2 9.9 %copy-start.5 = (f32[1,4,6]{2,1,0:T(4,128)S(1)}, f32[1,4,6]{2,1,0:T(4,128)}, u32[]{:S(2)}) copy-start(f32[1,4,6]{2,1,0:T(4,128)} %law_ref.1) | copy-start | bytes 292
  10.2 9.9 %copy-start.6 = (s32[1,2]{1,0:T(1,128)S(1)}, s32[1,2]{1,0:T(1,128)}, u32[]{:S(2)}) copy-start(s32[1,2]{1,0:T(1,128)} %count_ref) | copy-start | bytes 28
  10.3 9.9 %collective-permute-start.1 = (bf16[80,512]{1,0:T(8,128)(2,1)S(1)}, bf16[80,512]{1,0:T(8,128)(2,1)S(1)}, u32[]{:S(2)}, u32[]{:S(2)}) collective-permute-start(bf16[80,512]{1,0:T(8,128)(2,1)S(1)} %get-tuple-element.61.odd_ref), channel_id=1, source_target_pairs={{4,8},{12,16},{20,24},{28,32},{36,40},{44,48},{52,56},{60,64},{68,... | collective-permute-start | bytes 245768 | tf_op jit(solution)/shard_map/ppermute | solution.py:264
  12.6 7.6 %collective-permute-start.2 = (bf16[80,512]{1,0:T(8,128)(2,1)S(1)}, bf16[80,512]{1,0:T(8,128)(2,1)S(1)}, u32[]{:S(2)}, u32[]{:S(2)}) collective-permute-start(bf16[80,512]{1,0:T(8,128)(2,1)S(1)} %get-tuple-element.62.even_ref), channel_id=1, source_target_pairs={{0,4},{8,12},{16,20},{24,28},{32,36},{40,44},{48,52},{56,60},{64,6... | collective-permute-start | bytes 245768 | tf_op jit(solution)/shard_map/ppermute | solution.py:264
  18.2 4.4 %collective-permute-start.3 = (f32[8,128]{1,0:T(8,128)S(1)}, f32[8,128]{1,0:T(8,128)S(1)}, u32[]{:S(2)}, u32[]{:S(2)}) collective-permute-start(f32[8,128]{1,0:T(8,128)S(1)} %add.3.pair_ref), channel_id=1, source_target_pairs={{0,1},{2,3},{1,0},{3,2},{4,5},{6,7},{5,4},{7,6},{8,9},{10,11},{9,8... | collective-permute-start | bytes 12296 | tf_op jit(solution)/shard_map/ppermute | solution.py:264
  20.2 2.3 %copy-start.3 = (bf16[375,75]{0,1:T(8,128)(2,1)S(1)}, bf16[375,75]{0,1:T(8,128)(2,1)}, u32[]{:S(2)}) copy-start(bf16[375,75]{0,1:T(8,128)(2,1)} %param.21) | copy-start | bytes 168754
